TPU v7x, 768 devices: a whole 4x8x12 slice. The times are simulated.
768 devices in a mesh: dp: 24 (over z, core), row: 32 (over y, x).
Axes of the slice: x: 4, y: 8, z: 12, core: 2. Of those that a mesh axis runs over, the one named last changes fastest.
Arguments:
- user_table: bfloat16 [196608, 256], P('row'), may hold values from -1 to 1
- user_ids: int32 [3072, 32], P('dp'), may hold values from 0 to 196607
- item_features: bfloat16 [196608, 256], P(('dp', 'row')), may hold values from -6 to 6
- counts: int32 [32, 96], P('row'), may hold values from 1 to 512, 6144 in all within a row
- placement: int32 [32, 96], P('row'), may hold values from 0 to 95, each once within a row
- labels: int32 [196608], P(('dp', 'row')), may hold values 0 or 1
- w_hidden: bfloat16 [768, 1024], replicated, may hold values from -0.21875 to 0.21875
- bias: float32 [1024], replicated, may hold values from -3 to 3
- w_out: bfloat16 [1024], replicated, may hold values from -0.1875 to 0.1875
Outputs:
- table_grad: float32 [196608, 256], P(('row', 'dp'))
- item_grad: bfloat16 [196608, 256], P(('dp', 'row'))
Inputs may be any that keep to these rules, and one draw needn't show every extreme that they name: `counts`: each row sums to 6144. `placement`: each row is a permutation.
All inputs are finite; a program needn't handle non-finite values. No bound on the sum of `labels` on one device may be relied on, other than what follows from the above.
Results may differ from a plain program's by a relative error of at most 0.006.
Values may be sent and summed in bfloat16 or wider, within the bound.
A program may use at most 32 MiB of HBM per device.

v0:
```python
import jax
import jax.numpy as jnp
from jax import lax
from jax.sharding import PartitionSpec as P

loss_scale = 64.0


def tile_counts(bags, first, width):
    wanted = first + jnp.arange(width, dtype=jnp.int32)
    matches = bags[:, :, None] == wanted[None, None, :]
    return jnp.sum(matches.astype(jnp.float32), axis=1)


def per_device(
    user_table, user_ids, item_features, counts, placement, labels, w_hidden, bias, w_out
):
    table_rows = user_table.shape[0]
    width = user_table.shape[1]
    data_count = lax.axis_size("dp")
    shard_count = lax.axis_size("row")
    share = table_rows // data_count
    req_rows = user_ids.shape[0] // shard_count
    cand_rows = item_features.shape[0]
    column = counts.shape[1]
    data_index = lax.axis_index("dp")
    shard_index = lax.axis_index("row")
    table_base = shard_index * table_rows

    def add_tile(total, number):
        rows_part = lax.dynamic_slice_in_dim(user_table, number * share, share, 0)
        matches = tile_counts(user_ids, table_base + number * share, share).astype(jnp.bfloat16)
        return (total + jnp.dot(matches, rows_part, preferred_element_type=jnp.float32), None)

    total, _ = lax.scan(
        add_tile,
        jnp.zeros((req_rows * lax.axis_size("row"), width), jnp.float32),
        jnp.arange(data_count, dtype=jnp.int32),
    )
    pooled = lax.psum_scatter(total, "row", scatter_dimension=0, tiled=True).astype(jnp.bfloat16)
    column_counts = counts[0]
    order = placement[0]
    ordered = jnp.take(column_counts, order)
    before = jnp.cumsum(ordered) - ordered
    starts = jnp.zeros((column,), jnp.int32).at[order].set(before)
    slots = data_index * cand_rows + jnp.arange(cand_rows, dtype=jnp.int32)
    member = (
        (slots[:, None] >= starts[None, :]) & (slots[:, None] < (starts + column_counts)[None, :])
    ).astype(jnp.float32)
    member_half = member.astype(jnp.bfloat16)
    picked = member_half
    user_rows = jnp.dot(
        picked, lax.all_gather(pooled, "dp", axis=0, tiled=True), preferred_element_type=jnp.float32
    ).astype(jnp.bfloat16)
    both = (user_rows.astype(jnp.float32) * item_features.astype(jnp.float32)).astype(jnp.bfloat16)
    features = jnp.concatenate([user_rows, item_features, both], axis=1)
    pre = jnp.dot(features, w_hidden, preferred_element_type=jnp.float32) + bias
    hidden = jax.nn.silu(pre).astype(jnp.bfloat16)
    score = jnp.dot(hidden, w_out, preferred_element_type=jnp.float32)
    dscore = loss_scale * (jax.nn.sigmoid(score) - labels.astype(jnp.float32))
    sigma = jax.nn.sigmoid(pre)
    slope = sigma * (1.0 + pre * (1.0 - sigma))
    dhidden = (dscore[:, None] * w_out.astype(jnp.float32)[None, :] * slope).astype(jnp.bfloat16)
    dfeatures = lax.dot_general(
        dhidden, w_hidden, (((1,), (1,)), ((), ())), preferred_element_type=jnp.float32
    )
    item_grad = (
        dfeatures[:, width : 2 * width] + dfeatures[:, 2 * width :] * user_rows.astype(jnp.float32)
    ).astype(jnp.bfloat16)
    user_grad = dfeatures[:, :width] + dfeatures[:, 2 * width :] * item_features.astype(jnp.float32)
    picked = member
    request_grad = lax.psum_scatter(
        lax.dot_general(
            picked,
            user_grad,
            (((0,), (0,)), ((), ())),
            precision=lax.Precision.HIGHEST,
            preferred_element_type=jnp.float32,
        ),
        "dp",
        scatter_dimension=0,
        tiled=True,
    )
    group_grad = lax.all_gather(request_grad, "row", axis=0, tiled=True)

    def one_tile(number):
        matches = tile_counts(user_ids, table_base + number * share, share)
        return lax.dot_general(
            matches,
            group_grad,
            (((0,), (0,)), ((), ())),
            precision=lax.Precision.HIGHEST,
            preferred_element_type=jnp.float32,
        )

    pieces = lax.map(one_tile, jnp.arange(share * lax.axis_size("dp") // share, dtype=jnp.int32))
    table_grad = lax.psum_scatter(
        pieces.reshape(share * lax.axis_size("dp"), width), "dp", scatter_dimension=0, tiled=True
    )
    return (table_grad, item_grad)


def solution(mesh):
    return jax.shard_map(
        per_device,
        mesh=mesh,
        in_specs=(
            P("row", None),
            P("dp", None),
            P(("dp", "row"), None),
            P("row", None),
            P("row", None),
            P(("dp", "row")),
            P(),
            P(),
            P(),
        ),
        out_specs=(P(("row", "dp"), None), P(("dp", "row"), None)),
        check_vma=False,
    )
```

profile of v0, /device:TPU:1, one launch (start us, length us, event | category | flops | bytes accessed | tf_op | source)
XLA Modules:
  0.0 650.1 jit_solution(18170324679519398723)
XLA Ops:
  9.4 1.6 gather_fusion
  16.1 82.2 %while.22 = (s32[]{:T(128)}, f32[128,256]{1,0:T(8,128)S(1)}, s32[128,32]{1,0:T(8,128)S(1)}, s32[24]{0:T(128)S(1)}, s32[]{:T(128)}, /*index=5*/bf16[6144,256]{1,0...) while((s32[]{:T(128)}, f32[128,256]{1,0:T(8,128)S(1)}, s32[128,32]{1,0:T(8,128)S(1)}, ...), condition=%wide.region_4.5_spmd.clone, body=%wide.region_2.0_spmd.clone.sunk | while | flops 19955976 | bytes 542917 | solution.py:35
  98.3 116.6 %all-reduce.6 = bf16[128,256]{1,0:T(8,128)(2,1)S(1)} all-reduce(f32[128,256]{1,0:T(8,128)S(1)} %get-tuple-element.66), channel_id=2, replica_groups=mesh['dp'=24,'row'=32] {'row'}, use_global_device_ids=true, to_apply=%region_5.6.clone | all-reduce | flops 32768 | bytes 196608
  216.8 61.4 %all-gather = bf16[24,4,256]{2,1,0:T(4,128)(2,1)S(1)} all-gather(bf16[1,4,256]{2,1,0:T(4,128)(2,1)S(1)} %fusion.30), channel_id=1, replica_groups=mesh['dp'=24,'row'=32] {'dp'}, dimensions={0}, use_global_device_ids=true | all-gather | bytes 51200 | tf_op jit(solution)/shard_map/all_gather | solution.py:53
  283.4 138.9 %all-reduce.5.cloned.1.call-done = f32[96,256]{1,0:T(8,128)} async-done(((f32[96,256]{1,0:T(8,128)}), f32[96,256]{1,0:T(8,128)}) %all-reduce.5.cloned.1.call-update) | async-done | bytes 98320
  423.1 30.9 %all-gather.1 = f32[32,4,256]{2,1,0:T(4,128)S(1)} all-gather(f32[1,4,256]{2,1,0:T(4,128)S(1)} %dynamic-slice_bitcast_fusion), channel_id=1, replica_groups=mesh['dp'=24,'row'=32] {'row'}, dimensions={0}, use_global_device_ids=true | all-gather | bytes 135168 | tf_op jit(solution)/shard_map/all_gather | solution.py:84
  454.0 93.6 %while.21 = (s32[]{:T(128)}, f32[24,256,256]{2,1,0:T(8,128)}, s32[128,32]{1,0:T(8,128)S(1)}, s32[24]{0:T(128)S(1)}, s32[]{:T(128)}, /*index=5*/f32[128,256]{1,0:T(8,128)S(1)}, s32[]{:T(128)}, s32[1]{0:T(128)}) while((s32[]{:T(128)}, f32[24,256,256]{2,1,0:T(8,128)}, s32[128,32]{1,0:T(8,128)S(1)}, s32[24]{0:T(128)S(1)}, s32[]{:T(128)}, ...), condition=%wide.region_9.10_spmd, body=%wide.region_7.9_spmd.sunk | while | flops 103776512 | bytes 673929 | solution.py:96
  455.2 1.5 convert_reduce_fusion.4
  459.1 1.5 convert_reduce_fusion.4
  463.0 1.5 convert_reduce_fusion.4
  466.9 1.5 convert_reduce_fusion.4
  470.8 1.5 convert_reduce_fusion.4
  474.7 1.5 convert_reduce_fusion.4
  478.6 1.5 convert_reduce_fusion.4
  482.5 1.5 convert_reduce_fusion.4
  486.4 1.5 convert_reduce_fusion.4
  490.3 1.5 convert_reduce_fusion.4
  494.2 1.5 convert_reduce_fusion.4
  498.1 1.5 convert_reduce_fusion.4
  502.0 1.5 convert_reduce_fusion.4
  505.9 1.5 convert_reduce_fusion.4
  509.8 1.5 convert_reduce_fusion.4
  513.7 1.5 convert_reduce_fusion.4
  517.6 1.5 convert_reduce_fusion.4
  521.5 1.5 convert_reduce_fusion.4
  525.4 1.5 convert_reduce_fusion.4
  529.3 1.5 convert_reduce_fusion.4
  533.2 1.5 convert_reduce_fusion.4
  537.1 1.5 convert_reduce_fusion.4
  541.0 1.5 convert_reduce_fusion.4
  544.9 1.5 convert_reduce_fusion.4
  548.4 94.9 %reduce-scatter.2.cloned.1.call-done = f32[256,256]{1,0:T(8,128)} async-done(((f32[6144,256]{1,0:T(8,128)}), f32[256,256]{1,0:T(8,128)}) %reduce-scatter.2.cloned.1.call-update) | async-done | bytes 262160 | tf_op jit(solution)/shard_map/reduce_scatter | solution.py:97
  (210 shorter events, 120.3 us)
Async XLA Ops:
  7.2 271.4 %copy-start = (bf16[768,1024]{1,0:T(8,128)(2,1)S(1)}, bf16[768,1024]{1,0:T(8,128)(2,1)}, u32[]{:S(2)}) copy-start(bf16[768,1024]{1,0:T(8,128)(2,1)} %param.19) | copy-start | bytes 4718596
  7.2 271.4 %copy-start.1 = (f32[1024]{0:T(1024)S(1)}, f32[1024]{0:T(1024)}, u32[]{:S(2)}) copy-start(f32[1024]{0:T(1024)} %param.20) | copy-start | bytes 12292
  7.2 415.2 %all-reduce.5.cloned.1.call-start = ((), (), s32[]{:S(2)}) async-start(), calls=%async_computation.2 | async-start | bytes 196608
  98.3 181.2 %copy-start.2 = (s32[256]{0:T(256)S(1)}, s32[256]{0:T(256)}, u32[]{:S(2)}) copy-start(s32[256]{0:T(256)} %param.18) | copy-start | bytes 3076
  281.5 361.8 %reduce-scatter.2.cloned.1.call-start = ((), (), s32[]{:S(2)}) async-start(), calls=%async_computation.1 | async-start | bytes 6553600 | tf_op jit(solution)/shard_map/reduce_scatter | solution.py:97
Sparse Core Ops, SparseCore 0:
  281.6 140.7 all-reduce.4
  547.7 95.5 reduce-scatter.1
where the time goes:
time: 654 us; the launch traced here: 650 us
  waiting for transfers between devices  234 us (36%)
  blocking collectives  209 us (32%)
  other arithmetic  62.3 us (10%)
  matrix products  56.5 us (9%)
  local copies, waits for them, and re-layouts  39.2 us (6%)
  loops' own time  33.9 us (5%)
  between operations  15.5 us (2%)
    unnamed x3, waiting for transfers between devices  139 us
    unnamed x1, blocking collectives  117 us
    reduce_scatter x1, waiting for transfers between devices, per_device(): lax.psum_scatter(pieces.reshape(share * lax.axis_size('dp'), width), 'dp'...  94.9 us
    all_gather x1, blocking collectives, per_device(): lax.all_gather(pooled, 'dp', axis=0, tiled=True)  61.4 us
    reduce_sum x48, other arithmetic, tile_counts(): return jnp.sum(matches.astype(jnp.float32), axis=1)  58.3 us
    all_gather x1, blocking collectives, per_device(): group_grad = lax.all_gather(request_grad, 'row', axis=0, tiled=True)  30.9 us
    dynamic_slice x48, local copies, waits for them, and re-layouts, per_device(): lax.scan(add_tile, jnp.zeros((req_rows * lax.axis_size('row'), width), jn...  30 us
    dot_general x24, matrix products, one_tile(): lax.dot_general(matches, group_grad, (((0,), (0,)), ((), ())), precision=...  27.2 us
  transfers between devices with their start and end apart: 2, of which 2 were waited for; matrix products, arithmetic and copies ran while one was open for 0% of the time, Pallas kernels for 0%

commit v1 on v0

v1 whole, which is shorter than its diff:
```python
import functools

import jax
import jax.numpy as jnp
from jax import lax
from jax.experimental import pallas as pl
from jax.experimental.pallas import tpu as pltpu
from jax.sharding import PartitionSpec as P

MESH = pl.DeviceIdType.MESH
loss_scale = 64.0

N_DP = 24
N_ROW = 32
N_X = 4
N_Z = 12
REQ = 4
GROUP = N_ROW * REQ
COLUMN = N_DP * REQ
BAG = 32
E = 256
H = 1024
ROWS = 6144
SHARE = ROWS // N_DP
CAND = 256
QUARTER = GROUP // N_X
BLOCK = 16
N_BLOCK = GROUP // BLOCK
BF16 = jnp.bfloat16
F32 = jnp.float32


def iota(shape, dim, dtype=jnp.int32):
    return lax.broadcasted_iota(jnp.int32, shape, dim).astype(dtype)


def to_messages(rows):
    n = rows.shape[0] // 8
    left = rows[:, :128].reshape(n, 8, 128)
    right = rows[:, 128:].reshape(n, 8, 128)
    upper = iota((n, 8, 128), 1) < 4
    even = jnp.where(upper, left, pltpu.roll(right, 4, axis=1))
    odd = jnp.where(upper, pltpu.roll(left, 4, axis=1), right)
    return jnp.stack([even, odd], axis=1).reshape(2 * n, 8, 128)


def from_messages(messages):
    n = messages.shape[0] // 2
    pairs = messages.reshape(n, 2, 8, 128)
    even, odd = pairs[:, 0], pairs[:, 1]
    upper = iota((n, 8, 128), 1) < 4
    left = jnp.where(upper, even, pltpu.roll(odd, 4, axis=1))
    right = jnp.where(upper, pltpu.roll(even, 4, axis=1), odd)
    return left.reshape(8 * n, 128), right.reshape(8 * n, 128)


def kernel(
    table_hbm,
    ids_flat_ref,
    ids_turned_ref,
    item_ref,
    counts_ref,
    placement_ref,
    labels_ref,
    w_hidden_hbm,
    bias_ref,
    w_out_ref,
    table_grad_ref,
    item_grad_ref,
    table,
    w_hidden,
    group_counts,
    partial_out,
    partial_in,
    pooled_out,
    pooled_in,
    pooled_column,
    grad_out,
    grad_in,
    request_out,
    request_in,
    ids_all,
    own_counts,
    all_grads,
    load_sem,
    ids_send,
    ids_recv,
    partial_send,
    partial_recv,
    pooled_send,
    pooled_recv,
    grad_send,
    grad_recv,
    request_send,
    request_recv,
    z_send,
    z_recv,
    x_send,
    x_recv,
    core_send,
    core_recv,
):
    i = lax.axis_index("dp")
    k = lax.axis_index("row")
    z = i // 2
    core = i % 2
    y = k // N_X
    x = k % N_X

    table_load = pltpu.make_async_copy(table_hbm, table, load_sem.at[0])
    table_load.start()
    w_load = pltpu.make_async_copy(w_hidden_hbm, w_hidden, load_sem.at[1])
    w_load.start()

    barrier = pltpu.get_barrier_semaphore()

    def greet_row(s, _):
        pl.semaphore_signal(barrier, inc=1, device_id=(i, (k + s) % N_ROW), device_id_type=MESH)
        return 0

    def greet_dp(s, _):
        pl.semaphore_signal(barrier, inc=1, device_id=((i + s) % N_DP, k), device_id_type=MESH)
        return 0

    lax.fori_loop(1, N_ROW, greet_row, 0)
    lax.fori_loop(1, N_DP, greet_dp, 0)

    relative = ids_flat_ref[...] - k * ROWS
    inside = (relative >= 0) & (relative < ROWS)
    in_block = iota((N_BLOCK, BLOCK * BAG), 1) // BAG
    high_key = jnp.where(inside, (relative // SHARE) * BLOCK + in_block, -1)
    low_key = relative % SHARE
    high_row = iota((N_DP * BLOCK, 1), 0)
    low_row = iota((SHARE, 1), 0)
    for b in range(N_BLOCK):
        high = jnp.where(high_key[b : b + 1] == high_row, 1.0, 0.0).astype(BF16)
        low = jnp.where(low_key[b : b + 1] == low_row, 1.0, 0.0).astype(BF16)
        found = lax.dot_general(high, low, (((1,), (1,)), ((), ())), preferred_element_type=F32).astype(BF16)
        for h in range(N_DP):
            group_counts[b * BLOCK : (b + 1) * BLOCK, h * SHARE : (h + 1) * SHARE] = found[
                h * BLOCK : (h + 1) * BLOCK
            ]
    table_load.wait()
    partial = jnp.dot(group_counts[...], table[...], preferred_element_type=F32)
    partial_out[...] = to_messages(partial)

    pl.semaphore_wait(barrier, N_ROW - 1 + N_DP - 1)

    def row_copy(src, dst, send, recv, s):
        return pltpu.make_async_remote_copy(
            src_ref=src,
            dst_ref=dst,
            send_sem=send.at[s],
            recv_sem=recv.at[k],
            device_id=(i, (k + s) % N_ROW),
            device_id_type=MESH,
        )

    def dp_copy(src, dst, send, recv, s):
        return pltpu.make_async_remote_copy(
            src_ref=src,
            dst_ref=dst,
            send_sem=send.at[s],
            recv_sem=recv.at[i],
            device_id=((i + s) % N_DP, k),
            device_id_type=MESH,
        )

    def arrived(buffer, recv, source):
        pltpu.make_async_copy(buffer.at[source], buffer.at[source], recv.at[source]).wait()

    def send_partial(s, _):
        row_copy(partial_out.at[(k + s) % N_ROW], partial_in.at[k], partial_send, partial_recv, s).start()
        return 0

    lax.fori_loop(1, N_ROW, send_partial, 0)
    partial_in[k] = partial_out[k]

    ids_all[i] = ids_turned_ref[...]

    def send_ids(s, _):
        dp_copy(ids_turned_ref, ids_all.at[i], ids_send, ids_recv, s).start()
        return 0

    lax.fori_loop(1, N_DP, send_ids, 0)

    order = placement_ref[...]
    column_counts = counts_ref[...]
    eye = iota((128, 128), 0) == iota((128, 128), 1)
    place_at = jnp.where(order == iota((128, 128), 0), iota((128, 128), 1).astype(F32), 0.0)
    position = jnp.sum(place_at, axis=1, keepdims=True)
    position_row = jnp.sum(jnp.where(eye, position, 0.0), axis=0, keepdims=True)
    start = jnp.sum(jnp.where(position_row < position, column_counts, 0.0), axis=1, keepdims=True)
    count = jnp.sum(jnp.where(eye, column_counts, 0.0), axis=1, keepdims=True)
    start_row = jnp.sum(jnp.where(eye, start, 0.0), axis=0, keepdims=True)
    end, end_row = start + count, start_row + column_counts
    first = (i * CAND).astype(F32)
    slot = first + iota((CAND, 1), 0, F32)
    slot_row = first + iota((1, CAND), 1, F32)
    member = jnp.where((slot >= start_row) & (slot < end_row), 1.0, 0.0).astype(BF16)
    member_turned = jnp.where((slot_row >= start) & (slot_row < end), 1.0, 0.0).astype(BF16)
    diagonal = iota((CAND, CAND), 0) == iota((CAND, CAND), 1)
    label = jnp.sum(jnp.where(diagonal, labels_ref[...].astype(F32), 0.0), axis=1, keepdims=True)

    item = item_ref[...]
    item_wide = item.astype(F32)
    w_load.wait()
    item_pre = jnp.dot(item, w_hidden[E : 2 * E], preferred_element_type=F32) + bias_ref[...]

    def wait_partial(s, _):
        arrived(partial_in, partial_recv, (k + s) % N_ROW)
        return 0

    lax.fori_loop(1, N_ROW, wait_partial, 0)
    pooled = jnp.sum(partial_in[...], axis=0)
    pooled_out[...] = pooled
    pooled_in[i] = pooled

    def send_pooled(s, _):
        dp_copy(pooled_out, pooled_in.at[i], pooled_send, pooled_recv, s).start()
        return 0

    def wait_pooled(s, _):
        arrived(pooled_in, pooled_recv, (i + s) % N_DP)
        return 0

    lax.fori_loop(1, N_DP, send_pooled, 0)
    pooled_column[...] = jnp.zeros_like(pooled_column)
    lax.fori_loop(1, N_DP, wait_pooled, 0)
    left, right = from_messages(pooled_in[...])
    pooled_column[:COLUMN, :128] = left.astype(BF16)
    pooled_column[:COLUMN, 128:] = right.astype(BF16)

    user_rows = jnp.dot(member, pooled_column[...], preferred_element_type=F32)
    user = user_rows.astype(BF16)
    both = (user_rows * item_wide).astype(BF16)
    pre = (
        item_pre
        + jnp.dot(user, w_hidden[:E], preferred_element_type=F32)
        + jnp.dot(both, w_hidden[2 * E :], preferred_element_type=F32)
    )
    sigma = jax.nn.sigmoid(pre)
    hidden = (pre * sigma).astype(BF16).astype(F32)
    w_out = w_out_ref[...].astype(F32)
    score = jnp.sum(hidden * w_out, axis=1, keepdims=True)
    dscore = loss_scale * (jax.nn.sigmoid(score) - label)
    slope = sigma * (1.0 + pre * (1.0 - sigma))
    dhidden = (dscore * w_out * slope).astype(BF16)
    dfeatures = lax.dot_general(dhidden, w_hidden[...], (((1,), (1,)), ((), ())), preferred_element_type=F32)
    item_grad_ref[...] = (dfeatures[:, E : 2 * E] + dfeatures[:, 2 * E :] * user_rows).astype(BF16)
    user_grad = dfeatures[:, :E] + dfeatures[:, 2 * E :] * item_wide
    coarse = user_grad.astype(BF16)
    fine = (user_grad - coarse.astype(F32)).astype(BF16)
    column_grad = jnp.dot(member_turned, coarse, preferred_element_type=F32) + jnp.dot(
        member_turned, fine, preferred_element_type=F32
    )
    grad_out[...] = to_messages(column_grad[:COLUMN])

    def send_grad(s, _):
        dp_copy(grad_out.at[(i + s) % N_DP], grad_in.at[i], grad_send, grad_recv, s).start()
        return 0

    def wait_grad(s, _):
        arrived(grad_in, grad_recv, (i + s) % N_DP)
        return 0

    lax.fori_loop(1, N_DP, send_grad, 0)
    grad_in[i] = grad_out[i]
    lax.fori_loop(1, N_DP, wait_grad, 0)
    request_grad = jnp.sum(grad_in[...], axis=0)
    request_out[...] = request_grad
    request_in[k] = request_grad

    def send_request(s, _):
        row_copy(request_out, request_in.at[k], request_send, request_recv, s).start()
        return 0

    def wait_request(s, _):
        arrived(request_in, request_recv, (k + s) % N_ROW)
        return 0

    lax.fori_loop(1, N_ROW, send_request, 0)
    lax.fori_loop(1, N_ROW, wait_request, 0)
    left, right = from_messages(request_in[...])
    all_grads[z, core, :, :128] = left.astype(BF16)
    all_grads[z, core, :, 128:] = right.astype(BF16)

    def quarter(where, which):
        return all_grads.at[where, core, pl.ds(pl.multiple_of(which * QUARTER, QUARTER), QUARTER)]

    def send_z(s, _):
        pltpu.make_async_remote_copy(
            src_ref=quarter(z, x),
            dst_ref=quarter(z, x),
            send_sem=z_send.at[s],
            recv_sem=z_recv.at[z],
            device_id=(((z + s) % N_Z) * 2 + core, k),
            device_id_type=MESH,
        ).start()
        return 0

    lax.fori_loop(1, N_Z, send_z, 0)

    def x_copy(where, which, s):
        return pltpu.make_async_remote_copy(
            src_ref=quarter(where, which),
            dst_ref=quarter(where, which),
            send_sem=x_send.at[where, s],
            recv_sem=x_recv.at[where, which],
            device_id=(i, y * N_X + (x + s) % N_X),
            device_id_type=MESH,
        )

    def core_copy(where, side):
        return pltpu.make_async_remote_copy(
            src_ref=all_grads.at[where, side],
            dst_ref=all_grads.at[where, side],
            send_sem=core_send.at[where],
            recv_sem=core_recv.at[where],
            device_id=(z * 2 + 1 - core, k),
            device_id_type=MESH,
        )

    core_copy(z, core).start()

    own_first = k * ROWS + i * SHARE

    def count_group(group):
        ids = ids_all[group] - own_first
        row = iota((SHARE, GROUP), 0)
        total = jnp.zeros((SHARE, GROUP), F32)
        for b in range(BAG):
            total = total + jnp.where(ids[b : b + 1] == row, 1.0, 0.0)
        columns = pl.ds(pl.multiple_of(group * GROUP, GROUP), GROUP)
        own_counts[:, columns] = total.astype(BF16)

    def wait_ids(s, _):
        arrived(ids_all, ids_recv, (i + s) % N_DP)
        return 0

    lax.fori_loop(1, N_DP, wait_ids, 0)

    def pass_on(s, _):
        where = (z + s) % N_Z
        block = quarter(where, x)
        pltpu.make_async_copy(block, block, z_recv.at[where]).wait()
        for step in range(1, N_X):
            x_copy(where, x, step).start()
        count_group(2 * s)
        count_group(2 * s + 1)
        return 0

    lax.fori_loop(1, N_Z, pass_on, 0)
    count_group(0)
    count_group(1)

    def to_other_core(s, _):
        where = (z + s) % N_Z
        for step in range(1, N_X):
            which = (x + step) % N_X
            block = quarter(where, which)
            pltpu.make_async_copy(block, block, x_recv.at[where, which]).wait()
        core_copy(where, core).start()
        return 0

    lax.fori_loop(1, N_Z, to_other_core, 0)

    def wait_core(where, _):
        block = all_grads.at[where, 1 - core]
        pltpu.make_async_copy(block, block, core_recv.at[where]).wait()
        return 0

    lax.fori_loop(0, N_Z, wait_core, 0)
    table_grad_ref[...] = jnp.dot(
        own_counts[...], all_grads[...].reshape(N_DP * GROUP, E), preferred_element_type=F32
    )

    def drain_row(s, _):
        row_copy(partial_out.at[0], partial_in.at[k], partial_send, partial_recv, s).wait_send()
        row_copy(request_out, request_in.at[k], request_send, request_recv, s).wait_send()
        return 0

    def drain_dp(s, _):
        dp_copy(ids_turned_ref, ids_all.at[i], ids_send, ids_recv, s).wait_send()
        dp_copy(pooled_out, pooled_in.at[i], pooled_send, pooled_recv, s).wait_send()
        dp_copy(grad_out.at[0], grad_in.at[i], grad_send, grad_recv, s).wait_send()
        return 0

    def drain_z(s, _):
        block = quarter(z, x)
        pltpu.make_async_copy(block, block, z_send.at[s]).wait()
        where = (z + s) % N_Z
        for step in range(1, N_X):
            x_copy(where, x, step).wait_send()
        core_copy(where, core).wait_send()
        return 0

    lax.fori_loop(1, N_ROW, drain_row, 0)
    lax.fori_loop(1, N_DP, drain_dp, 0)
    lax.fori_loop(1, N_Z, drain_z, 0)
    core_copy(z, core).wait_send()


def per_device(user_table, user_ids, item_features, counts, placement, labels, w_hidden, bias, w_out):
    ids_flat = user_ids.reshape(N_BLOCK, BLOCK * BAG)
    ids_turned = user_ids.T
    pad = ((0, 0), (0, 128 - COLUMN))
    counts_row = jnp.pad(counts.astype(F32), pad)
    placement_row = jnp.pad(placement, pad, constant_values=-1)
    vmem = pl.BlockSpec(memory_space=pltpu.VMEM)
    hbm = pl.BlockSpec(memory_space=pl.ANY)
    dma = pltpu.SemaphoreType.DMA
    return pl.pallas_call(
        kernel,
        out_shape=(
            jax.ShapeDtypeStruct((SHARE, E), F32),
            jax.ShapeDtypeStruct((CAND, E), BF16),
        ),
        in_specs=[hbm, vmem, vmem, vmem, vmem, vmem, vmem, hbm, vmem, vmem],
        out_specs=(vmem, vmem),
        scratch_shapes=[
            pltpu.VMEM((ROWS, E), BF16),
            pltpu.VMEM((3 * E, H), BF16),
            pltpu.VMEM((GROUP, ROWS), BF16),
            pltpu.VMEM((N_ROW, 8, 128), F32),
            pltpu.VMEM((N_ROW, 8, 128), F32),
            pltpu.VMEM((8, 128), F32),
            pltpu.VMEM((N_DP, 8, 128), F32),
            pltpu.VMEM((128, E), BF16),
            pltpu.VMEM((N_DP, 8, 128), F32),
            pltpu.VMEM((N_DP, 8, 128), F32),
            pltpu.VMEM((8, 128), F32),
            pltpu.VMEM((N_ROW, 8, 128), F32),
            pltpu.VMEM((N_DP, BAG, GROUP), jnp.int32),
            pltpu.VMEM((SHARE, N_DP * GROUP), BF16),
            pltpu.VMEM((N_Z, 2, GROUP, E), BF16),
            dma((2,)),
            dma((N_DP,)),
            dma((N_DP,)),
            dma((N_ROW,)),
            dma((N_ROW,)),
            dma((N_DP,)),
            dma((N_DP,)),
            dma((N_DP,)),
            dma((N_DP,)),
            dma((N_ROW,)),
            dma((N_ROW,)),
            dma((N_Z,)),
            dma((N_Z,)),
            dma((N_Z, N_X)),
            dma((N_Z, N_X)),
            dma((N_Z,)),
            dma((N_Z,)),
        ],
        compiler_params=pltpu.CompilerParams(
            collective_id=0, has_side_effects=True, vmem_limit_bytes=48 * 1024 * 1024
        ),
    )(
        user_table,
        ids_flat,
        ids_turned,
        item_features,
        counts_row,
        placement_row,
        labels.reshape(1, CAND),
        w_hidden,
        bias.reshape(1, H),
        w_out.reshape(1, H),
    )


def solution(mesh):
    return jax.shard_map(
        per_device,
        mesh=mesh,
        in_specs=(
            P("row", None),
            P("dp", None),
            P(("dp", "row"), None),
            P("row", None),
            P("row", None),
            P(("dp", "row")),
            P(),
            P(),
            P(),
        ),
        out_specs=(P(("row", "dp"), None), P(("dp", "row"), None)),
        check_vma=False,
    )
```

time: 654 us -> 98.7 us (0.15)
  waiting for transfers between devices: 234 us -> 0 us
  blocking collectives: 209 us -> 0 us
  Pallas kernels: 0 us -> 87 us
  other arithmetic: 62.3 us -> 0.66 us
  matrix products: 56.5 us -> 0 us
  loops' own time: 33.9 us -> 0 us
  local copies, waits for them, and re-layouts: 39.2 us -> 9.89 us
  between operations: 15.5 us -> 0.66 us
    unnamed x3 -> x0, waiting for transfers between devices: 139 us -> none
    unnamed x1 -> x0, blocking collectives: 117 us -> none
    reduce_scatter x1 -> x0, waiting for transfers between devices: 94.9 us -> none  [per_device(): lax.psum_scatter(pieces.reshape(share * lax.axis_size('dp'), width), 'dp'...]
    all_gather x2 -> x0, blocking collectives: 92.2 us -> none  [the longest x1 61.4 us: per_device(): lax.all_gather(pooled, 'dp', axis=0, tiled=True)]
    pallas_call x0 -> x1, Pallas kernels: none -> 87 us  [per_device(): pl.pallas_call(kernel, out_shape=(jax.ShapeDtypeStruct((SHARE, E), F32),...]
    reduce_sum x48 -> x0, other arithmetic: 58.3 us -> none  [tile_counts(): return jnp.sum(matches.astype(jnp.float32), axis=1)]
    dot_general x53 -> x0, matrix products: 56.5 us -> none  [the longest x24 27.2 us: one_tile(): lax.dot_general(matches, group_grad, (((0,), (0,)), ((), ())), precision=...]
    another operation x2 -> x0, loops' own time: 33.9 us -> none  [the longest x1 17.8 us: per_device(): lax.scan(add_tile, jnp.zeros((req_rows * lax.axis_size('row'), width), jn...]
  transfers between devices with their start and end apart: 2 -> 0, of which waited for: 2 -> 0; matrix products, arithmetic and copies ran while one was open for 0% -> 0% of each run, Pallas kernels for 0% -> 0%
where the time goes in v1:
time: 98.7 us; the launch traced here: 98.2 us
  Pallas kernels  87 us (88%)
  local copies, waits for them, and re-layouts  9.89 us (10%)
    pallas_call x1, Pallas kernels, per_device(): pl.pallas_call(kernel, out_shape=(jax.ShapeDtypeStruct((SHARE, E), F32),...  87 us
    unnamed x15, local copies, waits for them, and re-layouts  8.45 us

profile of v1, /device:TPU:1, one launch (start us, length us, event | category | flops | bytes accessed | tf_op | source)
XLA Modules:
  0.0 98.2 jit_solution(15975346016450529214)
XLA Ops:
  0.6 0.7 convert_element_type.5
  1.3 0.7 pad.9.placement_ref
  2.0 0.7 reshape.19.w_out_ref
  2.6 0.8 copy.12
  3.5 0.1 reshape.16.ids_flat_ref
  3.5 0.0 copy-start
  3.6 1.9 %copy-done = bf16[6144,256]{1,0:T(8,128)(2,1)S(1)} copy-done((bf16[6144,256]{1,0:T(8,128)(2,1)S(1)}, bf16[6144,256]{1,0:T(8,128)(2,1)}, u32[]{:S(2)}) %copy-start) | copy-done | bytes 3145752
  5.4 0.0 copy-start.1
  5.4 1.4 %copy-done.1 = bf16[768,1024]{1,0:T(8,128)(2,1)S(1)} copy-done((bf16[768,1024]{1,0:T(8,128)(2,1)S(1)}, bf16[768,1024]{1,0:T(8,128)(2,1)}, u32[]{:S(2)}) %copy-start.1) | copy-done | bytes 1572888
  6.8 0.0 copy-start.2
  6.9 0.9 copy-done.2
  7.8 0.0 copy-start.3
  7.8 0.7 copy-done.3
  8.5 0.0 copy-start.4
  8.5 0.7 copy-done.4
  9.2 0.0 copy-start.5
  9.2 0.7 copy-done.5
  9.8 87.0 %shard_map.104 = (f32[256,256]{1,0:T(8,128)S(1)}, bf16[256,256]{1,0:T(8,128)(2,1)S(1)}) custom-call(bf16[6144,256]{1,0:T(8,128)(2,1)S(1)} %copy-done, s32[8,512]{1,0:T(8,128)S(1)} %reshape.16.ids_flat_ref, s32[32,128]{1,0:T(8,128)S(1)} %bitcast.3, bf16[256,256]{1,0:T(8,128)(2,1)S(1)} %copy-done.2, f32[1,128]{1,0:T(1,128)S(1)} %pad.8.counts_ref, ...), custom_call_target="tpu_custom_call" | custom-call | tf_op jit(solution)/shard_map/pallas_call | solution.py:413
  96.9 0.7 copy.15
  97.6 0.7 copy.16
  (1 shorter events, 0.0 us)
Async XLA Ops:
  3.5 1.9 %copy-start = (bf16[6144,256]{1,0:T(8,128)(2,1)S(1)}, bf16[6144,256]{1,0:T(8,128)(2,1)}, u32[]{:S(2)}) copy-start(bf16[6144,256]{1,0:T(8,128)(2,1)} %table_hbm.1) | copy-start | bytes 9437188
  5.4 1.4 %copy-start.1 = (bf16[768,1024]{1,0:T(8,128)(2,1)S(1)}, bf16[768,1024]{1,0:T(8,128)(2,1)}, u32[]{:S(2)}) copy-start(bf16[768,1024]{1,0:T(8,128)(2,1)} %w_hidden_hbm.1) | copy-start | bytes 4718596
  6.8 0.9 copy-start.2
  7.8 0.7 copy-start.3
  8.5 0.7 copy-start.4
  9.2 0.7 copy-start.5

commit v2 on v1

v2 whole, which is shorter than its diff:
```python
import functools

import jax
import jax.numpy as jnp
from jax import lax
from jax.experimental import pallas as pl
from jax.experimental.pallas import tpu as pltpu
from jax.sharding import PartitionSpec as P

MESH = pl.DeviceIdType.MESH
loss_scale = 64.0

N_DP = 24
N_ROW = 32
N_X = 4
N_Z = 12
REQ = 4
GROUP = N_ROW * REQ
COLUMN = N_DP * REQ
BAG = 32
E = 256
H = 1024
ROWS = 6144
SHARE = ROWS // N_DP
CAND = 256
QUARTER = GROUP // N_X
N_Y = N_ROW // N_X
BLOCK = 16
N_BLOCK = GROUP // BLOCK
BF16 = jnp.bfloat16
F32 = jnp.float32


def iota(shape, dim, dtype=jnp.int32):
    return lax.broadcasted_iota(jnp.int32, shape, dim).astype(dtype)


def to_messages(rows):
    n = rows.shape[0] // 8
    left = rows[:, :128].reshape(n, 8, 128)
    right = rows[:, 128:].reshape(n, 8, 128)
    upper = iota((n, 8, 128), 1) < 4
    even = jnp.where(upper, left, pltpu.roll(right, 4, axis=1))
    odd = jnp.where(upper, pltpu.roll(left, 4, axis=1), right)
    return jnp.stack([even, odd], axis=1).reshape(2 * n, 8, 128)


def from_messages(messages):
    n = messages.shape[0] // 2
    pairs = messages.reshape(n, 2, 8, 128)
    even, odd = pairs[:, 0], pairs[:, 1]
    upper = iota((n, 8, 128), 1) < 4
    left = jnp.where(upper, even, pltpu.roll(odd, 4, axis=1))
    right = jnp.where(upper, pltpu.roll(even, 4, axis=1), odd)
    return left.reshape(8 * n, 128), right.reshape(8 * n, 128)


def wrap(value, size):
    return jnp.where(value >= size, value - size, value)


def alternate(s, size):
    half = (s + 1) // 2
    return jnp.where(s % 2 == 1, half, wrap(size - half, size))


def flatten(turned):
    lag = (iota((8, 128), 0) + 8 - iota((8, 128), 1) // BLOCK) % 8
    parts = []
    for first in range(0, BAG, 8):
        tile = turned[first : first + 8]
        part = tile
        for d in range(1, 8):
            moved = pltpu.roll(pltpu.roll(tile, d, axis=0), 128 - BLOCK * d, axis=1)
            part = jnp.where(lag == d, moved, part)
        parts.append(part)
    return jnp.concatenate(parts, axis=1)


def kernel(
    table_hbm,
    ids_hbm,
    item_hbm,
    counts_hbm,
    placement_hbm,
    labels_hbm,
    w_hidden_hbm,
    bias_hbm,
    w_out_ref,
    table_grad_ref,
    item_grad_ref,
    table,
    w_hidden,
    ids_ref,
    item_ref,
    counts_ref,
    placement_ref,
    labels_ref,
    bias_ref,
    group_counts,
    partial_out,
    partial_in,
    pooled_out,
    pooled_in,
    pooled_column,
    grad_out,
    grad_core,
    grad_pair,
    grad_in,
    request_out,
    request_in,
    ids_all,
    own_counts,
    all_grads,
    load_sem,
    ids_send,
    ids_recv,
    partial_send,
    partial_recv,
    pooled_send,
    pooled_recv,
    grad_send,
    grad_recv,
    request_send,
    request_recv,
    z_send,
    z_recv,
    x_send,
    x_recv,
    core_send,
    core_recv,
):
    i = lax.axis_index("dp")
    k = lax.axis_index("row")
    z = i // 2
    core = i % 2
    y = k // N_X
    x = k % N_X

    ids_load = pltpu.make_async_copy(ids_hbm, ids_ref, load_sem.at[0])
    table_load = pltpu.make_async_copy(table_hbm, table, load_sem.at[1])
    later_loads = [
        pltpu.make_async_copy(source, target, load_sem.at[n])
        for n, (source, target) in enumerate(
            [
                (placement_hbm, placement_ref),
                (counts_hbm, counts_ref),
                (labels_hbm, labels_ref),
                (item_hbm, item_ref),
                (bias_hbm, bias_ref),
                (w_hidden_hbm, w_hidden),
            ],
            2,
        )
    ]
    ids_load.start()
    table_load.start()
    for load in later_loads:
        load.start()

    barrier = pltpu.get_barrier_semaphore()

    def greet_row(s, _):
        pl.semaphore_signal(barrier, inc=1, device_id=(i, (k + s) % N_ROW), device_id_type=MESH)
        return 0

    def greet_z(s, _):
        there = wrap(z + s, N_Z) * 2 + core
        pl.semaphore_signal(barrier, inc=1, device_id=(there, k), device_id_type=MESH)
        return 0

    lax.fori_loop(1, N_ROW, greet_row, 0)
    lax.fori_loop(1, N_Z, greet_z, 0)
    pl.semaphore_signal(barrier, inc=1, device_id=(z * 2 + 1 - core, k), device_id_type=MESH)

    ids_load.wait()
    relative = ids_ref[...] - k * ROWS
    relative = jnp.where((relative >= 0) & (relative < ROWS), relative, -1)
    flat = flatten(relative)
    in_block = iota((N_BLOCK, BLOCK * BAG), 1) % BLOCK
    high_key = jnp.where(flat >= 0, (flat >> 8) * BLOCK + in_block, -1)
    low_key = flat & (SHARE - 1)
    high_row = iota((N_DP * BLOCK, 1), 0)
    low_row = iota((SHARE, 1), 0)
    for b in range(N_BLOCK):
        high = jnp.where(high_key[b : b + 1] == high_row, 1.0, 0.0).astype(BF16)
        low = jnp.where(low_key[b : b + 1] == low_row, 1.0, 0.0).astype(BF16)
        found = lax.dot_general(high, low, (((1,), (1,)), ((), ())), preferred_element_type=F32).astype(BF16)
        for h in range(N_DP):
            group_counts[b * BLOCK : (b + 1) * BLOCK, h * SHARE : (h + 1) * SHARE] = found[
                h * BLOCK : (h + 1) * BLOCK
            ]
    table_load.wait()
    partial = jnp.dot(group_counts[...], table[...], preferred_element_type=F32)
    partial_out[...] = to_messages(partial)

    pl.semaphore_wait(barrier, N_ROW - 1 + N_Z)

    def row_copy(src, dst, send, recv, s):
        return pltpu.make_async_remote_copy(
            src_ref=src,
            dst_ref=dst,
            send_sem=send.at[s],
            recv_sem=recv.at[k],
            device_id=(i, (k + s) % N_ROW),
            device_id_type=MESH,
        )

    def z_copy(src, dst, send, recv, s):
        return pltpu.make_async_remote_copy(
            src_ref=src,
            dst_ref=dst,
            send_sem=send.at[s],
            recv_sem=recv.at[z],
            device_id=(wrap(z + s, N_Z) * 2 + core, k),
            device_id_type=MESH,
        )

    def core_copy(src, dst, n):
        return pltpu.make_async_remote_copy(
            src_ref=src,
            dst_ref=dst,
            send_sem=core_send.at[n],
            recv_sem=core_recv.at[n],
            device_id=(z * 2 + 1 - core, k),
            device_id_type=MESH,
        )

    def arrived(buffer, recv, source):
        pltpu.make_async_copy(buffer.at[source], buffer.at[source], recv.at[source]).wait()

    def send_partial(s, _):
        row_copy(partial_out.at[(k + s) % N_ROW], partial_in.at[k], partial_send, partial_recv, s).start()
        return 0

    lax.fori_loop(1, N_ROW, send_partial, 0)
    partial_in[k] = partial_out[k]

    to = iota((GROUP, GROUP), 1)
    moved_from = (to % QUARTER // REQ) * (N_X * REQ) + to // QUARTER * REQ + to % REQ
    reorder = jnp.where(iota((GROUP, GROUP), 0) == moved_from, 1.0, 0.0).astype(BF16)
    high_digit = (relative >> 8).astype(F32).astype(BF16)
    low_digit = (relative & (SHARE - 1)).astype(F32).astype(BF16)
    ids_moved = jnp.dot(high_digit, reorder, preferred_element_type=F32) * SHARE + jnp.dot(
        low_digit, reorder, preferred_element_type=F32
    )
    ids_all[core, z] = ids_moved.astype(jnp.int32).astype(jnp.int16)

    def send_ids(s, _):
        z_copy(ids_all.at[core, z], ids_all.at[core, z], ids_send, ids_recv, alternate(s, N_Z)).start()
        return 0

    lax.fori_loop(1, N_Z, send_ids, 0)

    own_first = i * SHARE

    def count_group(side, where):
        ids = jnp.clip(ids_all[side, where].astype(jnp.int32) - own_first, -1, SHARE).astype(F32)
        row = iota((SHARE, GROUP), 0, F32).astype(BF16)
        total = jnp.zeros((SHARE, GROUP), BF16)
        one, zero = jnp.ones((), BF16), jnp.zeros((), BF16)
        for b in range(BAG):
            wanted = jnp.broadcast_to(ids[b : b + 1], (16, GROUP)).astype(BF16)
            total = total + jnp.where(jnp.tile(wanted, (SHARE // 16, 1)) == row, one, zero)
        columns = pl.ds(pl.multiple_of((side * N_Z + where) * GROUP, GROUP), GROUP)
        own_counts[:, columns] = total

    def count_own_core(s, _):
        count_group(core, wrap(z + alternate(s, N_Z), N_Z))
        return 0

    def count_other_core(where, _):
        count_group(1 - core, where)
        return 0

    for load in later_loads:
        load.wait()
    padding = jnp.zeros((1, 128 - COLUMN), jnp.int32)
    order = jnp.concatenate([placement_ref[...], padding - 1], axis=1)
    column_counts = jnp.concatenate([counts_ref[...], padding], axis=1).astype(F32)
    eye = iota((128, 128), 0) == iota((128, 128), 1)
    place_at = jnp.where(order == iota((128, 128), 0), iota((128, 128), 1).astype(F32), 0.0)
    position = jnp.sum(place_at, axis=1, keepdims=True)
    position_row = jnp.sum(jnp.where(eye, position, 0.0), axis=0, keepdims=True)
    start = jnp.sum(jnp.where(position_row < position, column_counts, 0.0), axis=1, keepdims=True)
    count = jnp.sum(jnp.where(eye, column_counts, 0.0), axis=1, keepdims=True)
    start_row = jnp.sum(jnp.where(eye, start, 0.0), axis=0, keepdims=True)
    end, end_row = start + count, start_row + column_counts
    first = (i * CAND).astype(F32)
    slot = first + iota((CAND, 1), 0, F32)
    slot_row = first + iota((1, CAND), 1, F32)
    member = jnp.where((slot >= start_row) & (slot < end_row), 1.0, 0.0).astype(BF16)
    member_turned = jnp.where((slot_row >= start) & (slot_row < end), 1.0, 0.0).astype(BF16)
    diagonal = iota((CAND, CAND), 0) == iota((CAND, CAND), 1)
    label = jnp.sum(jnp.where(diagonal, labels_ref[...].astype(F32), 0.0), axis=1, keepdims=True)

    item = item_ref[...]
    item_wide = item.astype(F32)
    item_pre = jnp.dot(item, w_hidden[E : 2 * E], preferred_element_type=F32) + bias_ref[...]

    count_group(core, z)

    def wait_partial(s, _):
        arrived(partial_in, partial_recv, (k + s) % N_ROW)
        return 0

    lax.fori_loop(1, N_ROW, wait_partial, 0)
    pooled = jnp.sum(partial_in[...], axis=0)
    pooled_out[...] = pooled
    pooled_in[core, z] = pooled

    def send_pooled(s, _):
        z_copy(pooled_out, pooled_in.at[core, z], pooled_send, pooled_recv, alternate(s, N_Z)).start()
        return 0

    def wait_ids(s, _):
        where = wrap(z + s, N_Z)
        block = ids_all.at[core, where]
        pltpu.make_async_copy(block, block, ids_recv.at[where]).wait()
        return 0

    def wait_pooled(s, _):
        where = wrap(z + s, N_Z)
        block = pooled_in.at[core, where]
        pltpu.make_async_copy(block, block, pooled_recv.at[where]).wait()
        return 0

    lax.fori_loop(1, N_Z, send_pooled, 0)
    pooled_column[...] = jnp.zeros_like(pooled_column)
    lax.fori_loop(1, N_Z, wait_ids, 0)
    ids_over = core_copy(ids_all.at[core], ids_all.at[core], 0)
    ids_over.start()
    lax.fori_loop(1, 8, count_own_core, 0)
    lax.fori_loop(1, N_Z, wait_pooled, 0)
    pooled_over = core_copy(pooled_in.at[core], pooled_in.at[core], 1)
    pooled_over.start()
    pooled_over.wait_recv()
    pooled_all = jnp.stack([pooled_in[0], pooled_in[1]], axis=1).reshape(N_DP, 8, 128)
    left, right = from_messages(pooled_all)
    pooled_column[:COLUMN, :128] = left.astype(BF16)
    pooled_column[:COLUMN, 128:] = right.astype(BF16)

    user_rows = jnp.dot(member, pooled_column[...], preferred_element_type=F32)
    user = user_rows.astype(BF16)
    both = (user_rows * item_wide).astype(BF16)
    pre = (
        item_pre
        + jnp.dot(user, w_hidden[:E], preferred_element_type=F32)
        + jnp.dot(both, w_hidden[2 * E :], preferred_element_type=F32)
    )
    sigma = jax.nn.sigmoid(pre)
    hidden = (pre * sigma).astype(BF16).astype(F32)
    w_out = w_out_ref[...].astype(F32).reshape(1, H)
    score = jnp.sum(hidden * w_out, axis=1, keepdims=True)
    dscore = loss_scale * (jax.nn.sigmoid(score) - label)
    slope = sigma * (1.0 + pre * (1.0 - sigma))
    dhidden = (dscore * w_out * slope).astype(BF16)
    dfeatures = lax.dot_general(dhidden, w_hidden[...], (((1,), (1,)), ((), ())), preferred_element_type=F32)
    user_grad = dfeatures[:, :E] + dfeatures[:, 2 * E :] * item_wide
    coarse = user_grad.astype(BF16)
    fine = (user_grad - coarse.astype(F32)).astype(BF16)
    column_grad = jnp.dot(member_turned, coarse, preferred_element_type=F32) + jnp.dot(
        member_turned, fine, preferred_element_type=F32
    )
    by_core = to_messages(column_grad[:COLUMN]).reshape(N_Z, 2, 8, 128)
    grad_out[0] = by_core[:, 0]
    grad_out[1] = by_core[:, 1]

    grad_over = core_copy(grad_out.at[1 - core], grad_core, 2)
    grad_over.start()
    item_grad_ref[...] = (dfeatures[:, E : 2 * E] + dfeatures[:, 2 * E :] * user_rows).astype(BF16)
    grad_over.wait_recv()
    grad_pair[...] = grad_out[core] + grad_core[...]

    def send_grad(s, _):
        step = alternate(s, N_Z)
        z_copy(grad_pair.at[wrap(z + step, N_Z)], grad_in.at[z], grad_send, grad_recv, step).start()
        return 0

    def wait_grad(s, _):
        arrived(grad_in, grad_recv, wrap(z + s, N_Z))
        return 0

    lax.fori_loop(1, N_Z, send_grad, 0)
    grad_in[z] = grad_pair[z]
    lax.fori_loop(8, N_Z, count_own_core, 0)
    ids_over.wait_recv()
    lax.fori_loop(0, 6, count_other_core, 0)
    lax.fori_loop(1, N_Z, wait_grad, 0)
    request_grad = jnp.sum(grad_in[...], axis=0)
    request_out[...] = request_grad
    request_in[y] = request_grad

    def y_copy(s):
        return pltpu.make_async_remote_copy(
            src_ref=request_out,
            dst_ref=request_in.at[y],
            send_sem=request_send.at[s],
            recv_sem=request_recv.at[y],
            device_id=(i, (k + s * N_X) % N_ROW),
            device_id_type=MESH,
        )

    for s in range(1, N_Y):
        y_copy(s).start()
    lax.fori_loop(6, 9, count_other_core, 0)
    for s in range(1, N_Y):
        arrived(request_in, request_recv, (y + s) % N_Y)
    left, right = from_messages(request_in[...])
    own_rows = pl.ds(pl.multiple_of(x * QUARTER, QUARTER), QUARTER)
    all_grads[core, z, own_rows, :128] = left.astype(BF16)
    all_grads[core, z, own_rows, 128:] = right.astype(BF16)

    def quarter(where, which):
        return all_grads.at[core, where, pl.ds(pl.multiple_of(which * QUARTER, QUARTER), QUARTER)]

    def send_z(s, _):
        z_copy(quarter(z, x), quarter(z, x), z_send, z_recv, alternate(s, N_Z)).start()
        return 0

    def x_copy(where, which, s):
        return pltpu.make_async_remote_copy(
            src_ref=quarter(where, which),
            dst_ref=quarter(where, which),
            send_sem=x_send.at[where, s],
            recv_sem=x_recv.at[where, which],
            device_id=(i, y * N_X + (x + s) % N_X),
            device_id_type=MESH,
        )

    def grads_over(where, side):
        return core_copy(all_grads.at[side, where], all_grads.at[side, where], 3 + where)

    lax.fori_loop(1, N_Z, send_z, 0)
    for step in range(1, N_X):
        x_copy(z, x, step).start()
    lax.fori_loop(9, N_Z, count_other_core, 0)

    def pass_on(s, _):
        where = wrap(z + alternate(s, N_Z), N_Z)
        block = quarter(where, x)
        pltpu.make_async_copy(block, block, z_recv.at[where]).wait()
        for step in range(1, N_X):
            x_copy(where, x, step).start()
        return 0

    lax.fori_loop(1, N_Z, pass_on, 0)

    def to_other_core(s, _):
        where = wrap(z + alternate(s, N_Z), N_Z)
        for step in range(1, N_X):
            which = (x + step) % N_X
            block = quarter(where, which)
            pltpu.make_async_copy(block, block, x_recv.at[where, which]).wait()
        grads_over(where, core).start()
        return 0

    lax.fori_loop(0, N_Z, to_other_core, 0)

    def product(side):
        columns = pl.ds(pl.multiple_of(side * (N_Z * GROUP), N_Z * GROUP), N_Z * GROUP)
        rows = all_grads[side].reshape(N_Z * GROUP, E)
        return jnp.dot(own_counts[:, columns], rows, preferred_element_type=F32)

    own_side = product(core)

    def wait_core(where, _):
        grads_over(where, 1 - core).wait_recv()
        return 0

    lax.fori_loop(0, N_Z, wait_core, 0)
    table_grad_ref[...] = own_side + product(1 - core)

    def drain_row(s, _):
        row_copy(partial_out.at[0], partial_in.at[k], partial_send, partial_recv, s).wait_send()
        return 0

    def drain_z(s, _):
        z_copy(ids_all.at[core, z], ids_all.at[core, z], ids_send, ids_recv, s).wait_send()
        z_copy(pooled_out, pooled_in.at[core, z], pooled_send, pooled_recv, s).wait_send()
        z_copy(grad_pair.at[0], grad_in.at[z], grad_send, grad_recv, s).wait_send()
        z_copy(quarter(z, x), quarter(z, x), z_send, z_recv, s).wait_send()
        return 0

    def drain_x(where, _):
        for step in range(1, N_X):
            x_copy(where, x, step).wait_send()
        grads_over(where, core).wait_send()
        return 0

    for s in range(1, N_Y):
        y_copy(s).wait_send()
    lax.fori_loop(1, N_ROW, drain_row, 0)
    lax.fori_loop(1, N_Z, drain_z, 0)
    lax.fori_loop(0, N_Z, drain_x, 0)
    ids_over.wait_send()
    pooled_over.wait_send()
    grad_over.wait_send()


def hand_over(table_grad_hbm, item_grad_hbm, table_grad_out, item_grad_out, table_grad, item_grad, sem):
    parts = []
    for n, (source, held, target) in enumerate(
        [(table_grad_hbm, table_grad, table_grad_out), (item_grad_hbm, item_grad, item_grad_out)]
    ):
        for part in range(2):
            rows = pl.ds(part * 128, 128)
            parts.append(
                (
                    pltpu.make_async_copy(source.at[rows], held.at[rows], sem.at[0, n, part]),
                    pltpu.make_async_copy(held.at[rows], target.at[rows], sem.at[1, n, part]),
                )
            )
    for load, _ in parts:
        load.start()
    for load, store in parts:
        load.wait()
        store.start()
    for _, store in parts:
        store.wait()


def per_device(user_table, user_ids, item_features, counts, placement, labels, w_hidden, bias, w_out):
    vmem = pl.BlockSpec(memory_space=pltpu.VMEM)
    hbm = pl.BlockSpec(memory_space=pl.ANY)
    dma = pltpu.SemaphoreType.DMA
    outs = (jax.ShapeDtypeStruct((SHARE, E), F32), jax.ShapeDtypeStruct((CAND, E), BF16))
    grads = pl.pallas_call(
        kernel,
        out_shape=outs,
        in_specs=[hbm] * 8 + [vmem],
        out_specs=(vmem, vmem),
        scratch_shapes=[
            pltpu.VMEM((ROWS, E), BF16),
            pltpu.VMEM((3 * E, H), BF16),
            pltpu.VMEM((BAG, GROUP), jnp.int32),
            pltpu.VMEM((CAND, E), BF16),
            pltpu.VMEM((1, COLUMN), jnp.int32),
            pltpu.VMEM((1, COLUMN), jnp.int32),
            pltpu.VMEM((1, CAND), jnp.int32),
            pltpu.VMEM((1, H), F32),
            pltpu.VMEM((GROUP, ROWS), BF16),
            pltpu.VMEM((N_ROW, 8, 128), F32),
            pltpu.VMEM((N_ROW, 8, 128), F32),
            pltpu.VMEM((8, 128), F32),
            pltpu.VMEM((2, N_Z, 8, 128), F32),
            pltpu.VMEM((128, E), BF16),
            pltpu.VMEM((2, N_Z, 8, 128), F32),
            pltpu.VMEM((N_Z, 8, 128), F32),
            pltpu.VMEM((N_Z, 8, 128), F32),
            pltpu.VMEM((N_Z, 8, 128), F32),
            pltpu.VMEM((8, 128), F32),
            pltpu.VMEM((N_Y, 8, 128), F32),
            pltpu.VMEM((2, N_Z, BAG, GROUP), jnp.int16),
            pltpu.VMEM((SHARE, N_DP * GROUP), BF16),
            pltpu.VMEM((2, N_Z, GROUP, E), BF16),
            dma((8,)),
            dma((N_Z,)),
            dma((N_Z,)),
            dma((N_ROW,)),
            dma((N_ROW,)),
            dma((N_Z,)),
            dma((N_Z,)),
            dma((N_Z,)),
            dma((N_Z,)),
            dma((N_Y,)),
            dma((N_Y,)),
            dma((N_Z,)),
            dma((N_Z,)),
            dma((N_Z, N_X)),
            dma((N_Z, N_X)),
            dma((3 + N_Z,)),
            dma((3 + N_Z,)),
        ],
        compiler_params=pltpu.CompilerParams(
            collective_id=0, has_side_effects=True, vmem_limit_bytes=60 * 1024 * 1024
        ),
    )(
        user_table,
        user_ids.T,
        item_features,
        counts,
        placement,
        labels.reshape(1, CAND),
        w_hidden,
        bias.reshape(1, H),
        w_out,
    )
    return pl.pallas_call(
        hand_over,
        out_shape=outs,
        in_specs=[hbm] * 2,
        out_specs=(hbm, hbm),
        scratch_shapes=[pltpu.VMEM((SHARE, E), F32), pltpu.VMEM((CAND, E), BF16), dma((2, 2, 2))],
        compiler_params=pltpu.CompilerParams(vmem_limit_bytes=60 * 1024 * 1024),
    )(*grads)


def solution(mesh):
    return jax.shard_map(
        per_device,
        mesh=mesh,
        in_specs=(
            P("row", None),
            P("dp", None),
            P(("dp", "row"), None),
            P("row", None),
            P("row", None),
            P(("dp", "row")),
            P(),
            P(),
            P(),
        ),
        out_specs=(P(("row", "dp"), None), P(("dp", "row"), None)),
        check_vma=False,
    )
```

time: 98.7 us -> 69.8 us (0.71)
  Pallas kernels: 87 us -> 68.9 us
  local copies, waits for them, and re-layouts: 9.89 us -> 0 us
    pallas_call x1 -> x2, Pallas kernels: 87 us -> 68.9 us  [the longest x1 67.2 us: per_device(): pl.pallas_call(kernel, out_shape=outs, in_specs=[hbm] * 8 + [vmem], out_s...]
    unnamed x15 -> x0, local copies, waits for them, and re-layouts: 8.45 us -> none
where the time goes in v2:
time: 69.8 us; the launch traced here: 69.5 us
  Pallas kernels  68.9 us (99%)
    pallas_call x1, Pallas kernels, per_device(): pl.pallas_call(kernel, out_shape=outs, in_specs=[hbm] * 8 + [vmem], out_s...  67.2 us
    pallas_call x1, Pallas kernels, per_device(): pl.pallas_call(hand_over, out_shape=outs, in_specs=[hbm] * 2, out_specs=(...  1.73 us

profile of v2, /device:TPU:1, one launch (start us, length us, event | category | flops | bytes accessed | tf_op | source)
XLA Modules:
  0.0 69.5 jit_solution(4528403924699780012)
XLA Ops:
  0.6 67.2 %shard_map.104 = (f32[256,256]{1,0:T(8,128)}, bf16[256,256]{1,0:T(8,128)(2,1)}) custom-call(bf16[6144,256]{1,0:T(8,128)(2,1)} %table_hbm.1, s32[32,128]{1,0:T(8,128)} %bitcast.3, bf16[256,256]{1,0:T(8,128)(2,1)} %item_hbm.1, s32[1,96]{1,0:T(1,128)} %counts_hbm.1, s32[1,96]{1,0:T(1,128)} %placement_hbm.1, s32[1,256]{1,0:T(1,128)} %bitcast.5, ...), custom_call_target="tpu_custom_call" | custom-call | tf_op jit(solution)/shard_map/pallas_call | solution.py:528
  67.8 1.7 %shard_map.105 = (f32[256,256]{1,0:T(8,128)}, bf16[256,256]{1,0:T(8,128)(2,1)}) custom-call(f32[256,256]{1,0:T(8,128)} %get-tuple-element.4.table_grad_hbm, bf16[256,256]{1,0:T(8,128)(2,1)} %get-tuple-element.5.item_grad_hbm), custom_call_target="tpu_custom_call" | custom-call | tf_op jit(solution)/shard_map/pallas_call | solution.py:589

commit v3 on v2

--- a/solution.py
+++ b/solution.py
@@ -328,12 +328,12 @@
     lax.fori_loop(1, N_Z, send_pooled, 0)
     pooled_column[...] = jnp.zeros_like(pooled_column)
     lax.fori_loop(1, N_Z, wait_ids, 0)
-    ids_over = core_copy(ids_all.at[core], ids_all.at[core], 0)
-    ids_over.start()
     lax.fori_loop(1, 8, count_own_core, 0)
     lax.fori_loop(1, N_Z, wait_pooled, 0)
     pooled_over = core_copy(pooled_in.at[core], pooled_in.at[core], 1)
     pooled_over.start()
+    ids_over = core_copy(ids_all.at[core], ids_all.at[core], 0)
+    ids_over.start()
     pooled_over.wait_recv()
     pooled_all = jnp.stack([pooled_in[0], pooled_in[1]], axis=1).reshape(N_DP, 8, 128)
     left, right = from_messages(pooled_all)
@@ -415,47 +415,85 @@
         return all_grads.at[core, where, pl.ds(pl.multiple_of(which * QUARTER, QUARTER), QUARTER)]
 
     def send_z(s, _):
-        z_copy(quarter(z, x), quarter(z, x), z_send, z_recv, alternate(s, N_Z)).start()
-        return 0
-
-    def x_copy(where, which, s):
+        z_copy(quarter(z, x), quarter(z, x), z_send, z_recv, alternate(N_Z - s, N_Z)).start()
+        return 0
+
+    def half(where, which, part):
+        first = pl.multiple_of(which * QUARTER + part * (QUARTER // 2), QUARTER // 2)
+        return all_grads.at[core, where, pl.ds(first, QUARTER // 2)]
+
+    def x_copy(where, step):
+        side = (1 - step) // 2
         return pltpu.make_async_remote_copy(
-            src_ref=quarter(where, which),
-            dst_ref=quarter(where, which),
-            send_sem=x_send.at[where, s],
-            recv_sem=x_recv.at[where, which],
-            device_id=(i, y * N_X + (x + s) % N_X),
+            src_ref=quarter(where, x),
+            dst_ref=quarter(where, x),
+            send_sem=x_send.at[where, side],
+            recv_sem=x_recv.at[where, side],
+            device_id=(i, y * N_X + (x + step + N_X) % N_X),
             device_id_type=MESH,
         )
 
+    def x_wait(where, step):
+        side = (1 - step) // 2
+        block = quarter(where, (x - step + N_X) % N_X)
+        pltpu.make_async_copy(block, block, x_recv.at[where, side]).wait()
+
+    def x_pass(where, step):
+        side = (1 - step) // 2
+        block = half(where, (x - step + N_X) % N_X, side)
+        return pltpu.make_async_remote_copy(
+            src_ref=block,
+            dst_ref=block,
+            send_sem=x_send.at[where, 2 + side],
+            recv_sem=x_recv.at[where, 2 + side],
+            device_id=(i, y * N_X + (x + step + N_X) % N_X),
+            device_id_type=MESH,
+        )
+
+    def x_pass_wait(where, step):
+        side = (1 - step) // 2
+        block = half(where, (x + 2) % N_X, side)
+        pltpu.make_async_copy(block, block, x_recv.at[where, 2 + side]).wait()
+
     def grads_over(where, side):
         return core_copy(all_grads.at[side, where], all_grads.at[side, where], 3 + where)
 
+    def at_step(s):
+        return wrap(z + alternate(s, N_Z), N_Z)
+
+    def pass_on(where):
+        for step in (1, -1):
+            x_wait(where, step)
+            x_pass(where, step).start()
+
+    def to_other_core(where):
+        for step in (1, -1):
+            x_pass_wait(where, step)
+        grads_over(where, core).start()
+
     lax.fori_loop(1, N_Z, send_z, 0)
-    for step in range(1, N_X):
-        x_copy(z, x, step).start()
+    for step in (1, -1):
+        x_copy(z, step).start()
     lax.fori_loop(9, N_Z, count_other_core, 0)
 
-    def pass_on(s, _):
-        where = wrap(z + alternate(s, N_Z), N_Z)
+    def advance(s, _):
+        where = at_step(s)
         block = quarter(where, x)
         pltpu.make_async_copy(block, block, z_recv.at[where]).wait()
-        for step in range(1, N_X):
-            x_copy(where, x, step).start()
-        return 0
-
-    lax.fori_loop(1, N_Z, pass_on, 0)
-
-    def to_other_core(s, _):
-        where = wrap(z + alternate(s, N_Z), N_Z)
-        for step in range(1, N_X):
-            which = (x + step) % N_X
-            block = quarter(where, which)
-            pltpu.make_async_copy(block, block, x_recv.at[where, which]).wait()
-        grads_over(where, core).start()
-        return 0
-
-    lax.fori_loop(0, N_Z, to_other_core, 0)
+        for step in (1, -1):
+            x_copy(where, step).start()
+        pass_on(at_step(s - 1))
+
+        @pl.when(s >= 2)
+        def _():
+            to_other_core(at_step(s - 2))
+
+        return 0
+
+    lax.fori_loop(1, N_Z, advance, 0)
+    pass_on(at_step(N_Z - 1))
+    to_other_core(at_step(N_Z - 2))
+    to_other_core(at_step(N_Z - 1))
 
     def product(side):
         columns = pl.ds(pl.multiple_of(side * (N_Z * GROUP), N_Z * GROUP), N_Z * GROUP)
@@ -483,8 +521,9 @@
         return 0
 
     def drain_x(where, _):
-        for step in range(1, N_X):
-            x_copy(where, x, step).wait_send()
+        for step in (1, -1):
+            x_copy(where, step).wait_send()
+            x_pass(where, step).wait_send()
         grads_over(where, core).wait_send()
         return 0
 

time: 69.8 us -> 90.2 us (1.29); the launches traced: 69.5 us -> 89 us
  Pallas kernels: 68.9 us -> 88.3 us
    pallas_call x1, Pallas kernels: 67.2 us -> 86.6 us  [per_device(): pl.pallas_call(kernel, out_shape=outs, in_specs=[hbm] * 8 + [vmem], out_s...]
where the time goes in v3:
time: 90.2 us; the launch traced here: 89 us
  Pallas kernels  88.3 us (98%)
    pallas_call x1, Pallas kernels, per_device(): pl.pallas_call(kernel, out_shape=outs, in_specs=[hbm] * 8 + [vmem], out_s...  86.6 us

profile of v3, /device:TPU:1, one launch (start us, length us, event | category | flops | bytes accessed | tf_op | source)
XLA Modules:
  0.0 89.0 jit_solution(13324457205909995926)
XLA Ops:
  0.6 86.6 %shard_map.104 = (f32[256,256]{1,0:T(8,128)}, bf16[256,256]{1,0:T(8,128)(2,1)}) custom-call(bf16[6144,256]{1,0:T(8,128)(2,1)} %table_hbm.1, s32[32,128]{1,0:T(8,128)} %bitcast.3, bf16[256,256]{1,0:T(8,128)(2,1)} %item_hbm.1, s32[1,96]{1,0:T(1,128)} %counts_hbm.1, s32[1,96]{1,0:T(1,128)} %placement_hbm.1, s32[1,256]{1,0:T(1,128)} %bitcast.5, ...), custom_call_target="tpu_custom_call" | custom-call | tf_op jit(solution)/shard_map/pallas_call | solution.py:567
  87.2 1.7 %shard_map.105 = (f32[256,256]{1,0:T(8,128)}, bf16[256,256]{1,0:T(8,128)(2,1)}) custom-call(f32[256,256]{1,0:T(8,128)} %get-tuple-element.4.table_grad_hbm, bf16[256,256]{1,0:T(8,128)(2,1)} %get-tuple-element.5.item_grad_hbm), custom_call_target="tpu_custom_call" | custom-call | tf_op jit(solution)/shard_map/pallas_call | solution.py:628

commit v4 on v2

--- a/solution.py
+++ b/solution.py
@@ -33,6 +33,9 @@
 
 def iota(shape, dim, dtype=jnp.int32):
     return lax.broadcasted_iota(jnp.int32, shape, dim).astype(dtype)
+
+
+ROW_STEPS = [(v, u) for v in (4, 3, 5, 2, 6, 1, 7, 0) for u in (2, 1, 3, 0) if (v, u) != (0, 0)]
 
 
 def to_messages(rows):
@@ -160,17 +163,21 @@
 
     barrier = pltpu.get_barrier_semaphore()
 
-    def greet_row(s, _):
-        pl.semaphore_signal(barrier, inc=1, device_id=(i, (k + s) % N_ROW), device_id_type=MESH)
-        return 0
+    def in_row(step):
+        return (y + step[0]) % N_Y * N_X + (x + step[1]) % N_X
 
     def greet_z(s, _):
-        there = wrap(z + s, N_Z) * 2 + core
+        there = wrap(z + alternate(N_Z - s, N_Z), N_Z) * 2 + core
         pl.semaphore_signal(barrier, inc=1, device_id=(there, k), device_id_type=MESH)
         return 0
 
-    lax.fori_loop(1, N_ROW, greet_row, 0)
+    def greet_row(steps):
+        for step in steps:
+            pl.semaphore_signal(barrier, inc=1, device_id=(i, in_row(step)), device_id_type=MESH)
+
+    greet_row(ROW_STEPS[:12])
     lax.fori_loop(1, N_Z, greet_z, 0)
+    greet_row(ROW_STEPS[12:])
     pl.semaphore_signal(barrier, inc=1, device_id=(z * 2 + 1 - core, k), device_id_type=MESH)
 
     ids_load.wait()
@@ -196,13 +203,13 @@
 
     pl.semaphore_wait(barrier, N_ROW - 1 + N_Z)
 
-    def row_copy(src, dst, send, recv, s):
+    def row_copy(src, dst, send, recv, step):
         return pltpu.make_async_remote_copy(
             src_ref=src,
             dst_ref=dst,
-            send_sem=send.at[s],
+            send_sem=send.at[step[0] * N_X + step[1]],
             recv_sem=recv.at[k],
-            device_id=(i, (k + s) % N_ROW),
+            device_id=(i, in_row(step)),
             device_id_type=MESH,
         )
 
@@ -229,11 +236,8 @@
     def arrived(buffer, recv, source):
         pltpu.make_async_copy(buffer.at[source], buffer.at[source], recv.at[source]).wait()
 
-    def send_partial(s, _):
-        row_copy(partial_out.at[(k + s) % N_ROW], partial_in.at[k], partial_send, partial_recv, s).start()
-        return 0
-
-    lax.fori_loop(1, N_ROW, send_partial, 0)
+    for step in ROW_STEPS:
+        row_copy(partial_out.at[in_row(step)], partial_in.at[k], partial_send, partial_recv, step).start()
     partial_in[k] = partial_out[k]
 
     to = iota((GROUP, GROUP), 1)
@@ -310,7 +314,7 @@
     pooled_in[core, z] = pooled
 
     def send_pooled(s, _):
-        z_copy(pooled_out, pooled_in.at[core, z], pooled_send, pooled_recv, alternate(s, N_Z)).start()
+        z_copy(pooled_out, pooled_in.at[core, z], pooled_send, pooled_recv, alternate(N_Z - s, N_Z)).start()
         return 0
 
     def wait_ids(s, _):
@@ -328,12 +332,12 @@
     lax.fori_loop(1, N_Z, send_pooled, 0)
     pooled_column[...] = jnp.zeros_like(pooled_column)
     lax.fori_loop(1, N_Z, wait_ids, 0)
-    ids_over = core_copy(ids_all.at[core], ids_all.at[core], 0)
-    ids_over.start()
     lax.fori_loop(1, 8, count_own_core, 0)
     lax.fori_loop(1, N_Z, wait_pooled, 0)
     pooled_over = core_copy(pooled_in.at[core], pooled_in.at[core], 1)
     pooled_over.start()
+    ids_over = core_copy(ids_all.at[core], ids_all.at[core], 0)
+    ids_over.start()
     pooled_over.wait_recv()
     pooled_all = jnp.stack([pooled_in[0], pooled_in[1]], axis=1).reshape(N_DP, 8, 128)
     left, right = from_messages(pooled_all)
@@ -373,7 +377,7 @@
     grad_pair[...] = grad_out[core] + grad_core[...]
 
     def send_grad(s, _):
-        step = alternate(s, N_Z)
+        step = alternate(N_Z - s, N_Z)
         z_copy(grad_pair.at[wrap(z + step, N_Z)], grad_in.at[z], grad_send, grad_recv, step).start()
         return 0
 
@@ -401,7 +405,7 @@
             device_id_type=MESH,
         )
 
-    for s in range(1, N_Y):
+    for s in (4, 3, 5, 2, 6, 1, 7):
         y_copy(s).start()
     lax.fori_loop(6, 9, count_other_core, 0)
     for s in range(1, N_Y):
@@ -471,10 +475,6 @@
     lax.fori_loop(0, N_Z, wait_core, 0)
     table_grad_ref[...] = own_side + product(1 - core)
 
-    def drain_row(s, _):
-        row_copy(partial_out.at[0], partial_in.at[k], partial_send, partial_recv, s).wait_send()
-        return 0
-
     def drain_z(s, _):
         z_copy(ids_all.at[core, z], ids_all.at[core, z], ids_send, ids_recv, s).wait_send()
         z_copy(pooled_out, pooled_in.at[core, z], pooled_send, pooled_recv, s).wait_send()
@@ -490,7 +490,8 @@
 
     for s in range(1, N_Y):
         y_copy(s).wait_send()
-    lax.fori_loop(1, N_ROW, drain_row, 0)
+    for step in ROW_STEPS:
+        row_copy(partial_out.at[0], partial_in.at[k], partial_send, partial_recv, step).wait_send()
     lax.fori_loop(1, N_Z, drain_z, 0)
     lax.fori_loop(0, N_Z, drain_x, 0)
     ids_over.wait_send()

time: 69.8 us -> 67.5 us (0.967)
  Pallas kernels: 68.9 us -> 66.6 us
    pallas_call x1, Pallas kernels: 67.2 us -> 64.9 us  [per_device(): pl.pallas_call(kernel, out_shape=outs, in_specs=[hbm] * 8 + [vmem], out_s...]
where the time goes in v4:
time: 67.5 us; the launch traced here: 67.3 us
  Pallas kernels  66.6 us (99%)
    pallas_call x1, Pallas kernels, per_device(): pl.pallas_call(kernel, out_shape=outs, in_specs=[hbm] * 8 + [vmem], out_s...  64.9 us
    pallas_call x1, Pallas kernels, per_device(): pl.pallas_call(hand_over, out_shape=outs, in_specs=[hbm] * 2, out_specs=(...  1.73 us

profile of v4, /device:TPU:1, one launch (start us, length us, event | category | flops | bytes accessed | tf_op | source)
XLA Modules:
  0.0 67.3 jit_solution(9129642746410395812)
XLA Ops:
  0.6 64.9 %shard_map.104 = (f32[256,256]{1,0:T(8,128)}, bf16[256,256]{1,0:T(8,128)(2,1)}) custom-call(bf16[6144,256]{1,0:T(8,128)(2,1)} %table_hbm.1, s32[32,128]{1,0:T(8,128)} %bitcast.3, bf16[256,256]{1,0:T(8,128)(2,1)} %item_hbm.1, s32[1,96]{1,0:T(1,128)} %counts_hbm.1, s32[1,96]{1,0:T(1,128)} %placement_hbm.1, s32[1,256]{1,0:T(1,128)} %bitcast.5, ...), custom_call_target="tpu_custom_call" | custom-call | tf_op jit(solution)/shard_map/pallas_call | solution.py:529
  65.5 1.7 %shard_map.105 = (f32[256,256]{1,0:T(8,128)}, bf16[256,256]{1,0:T(8,128)(2,1)}) custom-call(f32[256,256]{1,0:T(8,128)} %get-tuple-element.4.table_grad_hbm, bf16[256,256]{1,0:T(8,128)(2,1)} %get-tuple-element.5.item_grad_hbm), custom_call_target="tpu_custom_call" | custom-call | tf_op jit(solution)/shard_map/pallas_call | solution.py:590

commit v5 on v4

--- a/solution.py
+++ b/solution.py
@@ -113,8 +113,11 @@
     request_out,
     request_in,
     ids_all,
-    own_counts,
+    chip_counts,
     all_grads,
+    parts,
+    part_out,
+    part_in,
     load_sem,
     ids_send,
     ids_recv,
@@ -248,33 +251,29 @@
     ids_moved = jnp.dot(high_digit, reorder, preferred_element_type=F32) * SHARE + jnp.dot(
         low_digit, reorder, preferred_element_type=F32
     )
-    ids_all[core, z] = ids_moved.astype(jnp.int32).astype(jnp.int16)
+    ids_all[z] = ids_moved.astype(jnp.int32).astype(jnp.int16)
 
     def send_ids(s, _):
-        z_copy(ids_all.at[core, z], ids_all.at[core, z], ids_send, ids_recv, alternate(s, N_Z)).start()
+        z_copy(ids_all.at[z], ids_all.at[z], ids_send, ids_recv, alternate(s, N_Z)).start()
         return 0
 
     lax.fori_loop(1, N_Z, send_ids, 0)
 
-    own_first = i * SHARE
-
-    def count_group(side, where):
-        ids = jnp.clip(ids_all[side, where].astype(jnp.int32) - own_first, -1, SHARE).astype(F32)
+    def count_group(n):
+        where, side = wrap(z + alternate(n // 2, N_Z), N_Z), n % 2
+        first = (z * 2 + side) * SHARE
+        ids = jnp.clip(ids_all[where].astype(jnp.int32) - first, -1, SHARE).astype(F32)
         row = iota((SHARE, GROUP), 0, F32).astype(BF16)
         total = jnp.zeros((SHARE, GROUP), BF16)
         one, zero = jnp.ones((), BF16), jnp.zeros((), BF16)
         for b in range(BAG):
             wanted = jnp.broadcast_to(ids[b : b + 1], (16, GROUP)).astype(BF16)
             total = total + jnp.where(jnp.tile(wanted, (SHARE // 16, 1)) == row, one, zero)
-        columns = pl.ds(pl.multiple_of((side * N_Z + where) * GROUP, GROUP), GROUP)
-        own_counts[:, columns] = total
-
-    def count_own_core(s, _):
-        count_group(core, wrap(z + alternate(s, N_Z), N_Z))
-        return 0
-
-    def count_other_core(where, _):
-        count_group(1 - core, where)
+        columns = pl.ds(pl.multiple_of(where * GROUP, GROUP), GROUP)
+        chip_counts[side, :, columns] = total
+
+    def count_step(n, _):
+        count_group(n)
         return 0
 
     for load in later_loads:
@@ -302,7 +301,7 @@
     item_wide = item.astype(F32)
     item_pre = jnp.dot(item, w_hidden[E : 2 * E], preferred_element_type=F32) + bias_ref[...]
 
-    count_group(core, z)
+    lax.fori_loop(0, 2, count_step, 0)
 
     def wait_partial(s, _):
         arrived(partial_in, partial_recv, (k + s) % N_ROW)
@@ -319,8 +318,7 @@
 
     def wait_ids(s, _):
         where = wrap(z + s, N_Z)
-        block = ids_all.at[core, where]
-        pltpu.make_async_copy(block, block, ids_recv.at[where]).wait()
+        arrived(ids_all, ids_recv, where)
         return 0
 
     def wait_pooled(s, _):
@@ -332,12 +330,10 @@
     lax.fori_loop(1, N_Z, send_pooled, 0)
     pooled_column[...] = jnp.zeros_like(pooled_column)
     lax.fori_loop(1, N_Z, wait_ids, 0)
-    lax.fori_loop(1, 8, count_own_core, 0)
+    lax.fori_loop(2, 11, count_step, 0)
     lax.fori_loop(1, N_Z, wait_pooled, 0)
     pooled_over = core_copy(pooled_in.at[core], pooled_in.at[core], 1)
     pooled_over.start()
-    ids_over = core_copy(ids_all.at[core], ids_all.at[core], 0)
-    ids_over.start()
     pooled_over.wait_recv()
     pooled_all = jnp.stack([pooled_in[0], pooled_in[1]], axis=1).reshape(N_DP, 8, 128)
     left, right = from_messages(pooled_all)
@@ -387,9 +383,7 @@
 
     lax.fori_loop(1, N_Z, send_grad, 0)
     grad_in[z] = grad_pair[z]
-    lax.fori_loop(8, N_Z, count_own_core, 0)
-    ids_over.wait_recv()
-    lax.fori_loop(0, 6, count_other_core, 0)
+    lax.fori_loop(11, 19, count_step, 0)
     lax.fori_loop(1, N_Z, wait_grad, 0)
     request_grad = jnp.sum(grad_in[...], axis=0)
     request_out[...] = request_grad
@@ -407,16 +401,16 @@
 
     for s in (4, 3, 5, 2, 6, 1, 7):
         y_copy(s).start()
-    lax.fori_loop(6, 9, count_other_core, 0)
+    lax.fori_loop(19, 22, count_step, 0)
     for s in range(1, N_Y):
         arrived(request_in, request_recv, (y + s) % N_Y)
     left, right = from_messages(request_in[...])
     own_rows = pl.ds(pl.multiple_of(x * QUARTER, QUARTER), QUARTER)
-    all_grads[core, z, own_rows, :128] = left.astype(BF16)
-    all_grads[core, z, own_rows, 128:] = right.astype(BF16)
+    all_grads[z, own_rows, :128] = left.astype(BF16)
+    all_grads[z, own_rows, 128:] = right.astype(BF16)
 
     def quarter(where, which):
-        return all_grads.at[core, where, pl.ds(pl.multiple_of(which * QUARTER, QUARTER), QUARTER)]
+        return all_grads.at[where, pl.ds(pl.multiple_of(which * QUARTER, QUARTER), QUARTER)]
 
     def send_z(s, _):
         z_copy(quarter(z, x), quarter(z, x), z_send, z_recv, alternate(s, N_Z)).start()
@@ -432,13 +426,10 @@
             device_id_type=MESH,
         )
 
-    def grads_over(where, side):
-        return core_copy(all_grads.at[side, where], all_grads.at[side, where], 3 + where)
-
     lax.fori_loop(1, N_Z, send_z, 0)
     for step in range(1, N_X):
         x_copy(z, x, step).start()
-    lax.fori_loop(9, N_Z, count_other_core, 0)
+    lax.fori_loop(22, 24, count_step, 0)
 
     def pass_on(s, _):
         where = wrap(z + alternate(s, N_Z), N_Z)
@@ -450,33 +441,36 @@
 
     lax.fori_loop(1, N_Z, pass_on, 0)
 
-    def to_other_core(s, _):
+    def product(where, side):
+        columns = pl.ds(pl.multiple_of(where * GROUP, GROUP), GROUP)
+        return jnp.dot(chip_counts[side, :, columns], all_grads[where], preferred_element_type=F32)
+
+    def wait_x(s):
         where = wrap(z + alternate(s, N_Z), N_Z)
         for step in range(1, N_X):
             which = (x + step) % N_X
             block = quarter(where, which)
             pltpu.make_async_copy(block, block, x_recv.at[where, which]).wait()
-        grads_over(where, core).start()
-        return 0
-
-    lax.fori_loop(0, N_Z, to_other_core, 0)
-
-    def product(side):
-        columns = pl.ds(pl.multiple_of(side * (N_Z * GROUP), N_Z * GROUP), N_Z * GROUP)
-        rows = all_grads[side].reshape(N_Z * GROUP, E)
-        return jnp.dot(own_counts[:, columns], rows, preferred_element_type=F32)
-
-    own_side = product(core)
-
-    def wait_core(where, _):
-        grads_over(where, 1 - core).wait_recv()
-        return 0
-
-    lax.fori_loop(0, N_Z, wait_core, 0)
-    table_grad_ref[...] = own_side + product(1 - core)
+        return where
+
+    def add_group(s, _):
+        where = wait_x(s)
+        for side in range(2):
+            parts[side] = parts[side] + product(where, side)
+        return 0
+
+    parts[...] = jnp.zeros_like(parts)
+    lax.fori_loop(0, N_Z - 1, add_group, 0)
+    last = wait_x(N_Z - 1)
+    part_out[...] = (parts[1 - core] + product(last, 1 - core)).astype(BF16)
+    part_over = core_copy(part_out, part_in, 3)
+    part_over.start()
+    own_part = parts[core] + product(last, core)
+    part_over.wait_recv()
+    table_grad_ref[...] = own_part + part_in[...].astype(F32)
 
     def drain_z(s, _):
-        z_copy(ids_all.at[core, z], ids_all.at[core, z], ids_send, ids_recv, s).wait_send()
+        z_copy(ids_all.at[z], ids_all.at[z], ids_send, ids_recv, s).wait_send()
         z_copy(pooled_out, pooled_in.at[core, z], pooled_send, pooled_recv, s).wait_send()
         z_copy(grad_pair.at[0], grad_in.at[z], grad_send, grad_recv, s).wait_send()
         z_copy(quarter(z, x), quarter(z, x), z_send, z_recv, s).wait_send()
@@ -485,7 +479,6 @@
     def drain_x(where, _):
         for step in range(1, N_X):
             x_copy(where, x, step).wait_send()
-        grads_over(where, core).wait_send()
         return 0
 
     for s in range(1, N_Y):
@@ -494,7 +487,7 @@
         row_copy(partial_out.at[0], partial_in.at[k], partial_send, partial_recv, step).wait_send()
     lax.fori_loop(1, N_Z, drain_z, 0)
     lax.fori_loop(0, N_Z, drain_x, 0)
-    ids_over.wait_send()
+    part_over.wait_send()
     pooled_over.wait_send()
     grad_over.wait_send()
 
@@ -552,9 +545,12 @@
             pltpu.VMEM((N_Z, 8, 128), F32),
             pltpu.VMEM((8, 128), F32),
             pltpu.VMEM((N_Y, 8, 128), F32),
-            pltpu.VMEM((2, N_Z, BAG, GROUP), jnp.int16),
-            pltpu.VMEM((SHARE, N_DP * GROUP), BF16),
-            pltpu.VMEM((2, N_Z, GROUP, E), BF16),
+            pltpu.VMEM((N_Z, BAG, GROUP), jnp.int16),
+            pltpu.VMEM((2, SHARE, N_Z * GROUP), BF16),
+            pltpu.VMEM((N_Z, GROUP, E), BF16),
+            pltpu.VMEM((2, SHARE, E), F32),
+            pltpu.VMEM((SHARE, E), BF16),
+            pltpu.VMEM((SHARE, E), BF16),
             dma((8,)),
             dma((N_Z,)),
             dma((N_Z,)),
@@ -570,8 +566,8 @@
             dma((N_Z,)),
             dma((N_Z, N_X)),
             dma((N_Z, N_X)),
-            dma((3 + N_Z,)),
-            dma((3 + N_Z,)),
+            dma((4,)),
+            dma((4,)),
         ],
         compiler_params=pltpu.CompilerParams(
             collective_id=0, has_side_effects=True, vmem_limit_bytes=60 * 1024 * 1024

time: 67.5 us -> 66.6 us (0.987)
  Pallas kernels: 66.6 us -> 65.7 us
    pallas_call x1, Pallas kernels: 64.9 us -> 64 us  [per_device(): pl.pallas_call(kernel, out_shape=outs, in_specs=[hbm] * 8 + [vmem], out_s...]
where the time goes in v5:
time: 66.6 us; the launch traced here: 66.4 us
  Pallas kernels  65.7 us (99%)
    pallas_call x1, Pallas kernels, per_device(): pl.pallas_call(kernel, out_shape=outs, in_specs=[hbm] * 8 + [vmem], out_s...  64 us
    pallas_call x1, Pallas kernels, per_device(): pl.pallas_call(hand_over, out_shape=outs, in_specs=[hbm] * 2, out_specs=(...  1.73 us

profile of v5, /device:TPU:1, one launch (start us, length us, event | category | flops | bytes accessed | tf_op | source)
XLA Modules:
  0.0 66.4 jit_solution(4040510578923610978)
XLA Ops:
  0.6 64.0 %shard_map.104 = (f32[256,256]{1,0:T(8,128)}, bf16[256,256]{1,0:T(8,128)(2,1)}) custom-call(bf16[6144,256]{1,0:T(8,128)(2,1)} %table_hbm.1, s32[32,128]{1,0:T(8,128)} %bitcast.3, bf16[256,256]{1,0:T(8,128)(2,1)} %item_hbm.1, s32[1,96]{1,0:T(1,128)} %counts_hbm.1, s32[1,96]{1,0:T(1,128)} %placement_hbm.1, s32[1,256]{1,0:T(1,128)} %bitcast.5, ...), custom_call_target="tpu_custom_call" | custom-call | tf_op jit(solution)/shard_map/pallas_call | solution.py:522
  64.6 1.7 %shard_map.105 = (f32[256,256]{1,0:T(8,128)}, bf16[256,256]{1,0:T(8,128)(2,1)}) custom-call(f32[256,256]{1,0:T(8,128)} %get-tuple-element.4.table_grad_hbm, bf16[256,256]{1,0:T(8,128)(2,1)} %get-tuple-element.5.item_grad_hbm), custom_call_target="tpu_custom_call" | custom-call | tf_op jit(solution)/shard_map/pallas_call | solution.py:586

commit v6 on v5

--- a/solution.py
+++ b/solution.py
@@ -90,6 +90,8 @@
     w_hidden_hbm,
     bias_hbm,
     w_out_ref,
+    table_grad_hbm,
+    item_grad_hbm,
     table_grad_ref,
     item_grad_ref,
     table,
@@ -119,6 +121,7 @@
     part_out,
     part_in,
     load_sem,
+    store_sem,
     ids_send,
     ids_recv,
     partial_send,
@@ -330,7 +333,7 @@
     lax.fori_loop(1, N_Z, send_pooled, 0)
     pooled_column[...] = jnp.zeros_like(pooled_column)
     lax.fori_loop(1, N_Z, wait_ids, 0)
-    lax.fori_loop(2, 11, count_step, 0)
+    lax.fori_loop(2, 12, count_step, 0)
     lax.fori_loop(1, N_Z, wait_pooled, 0)
     pooled_over = core_copy(pooled_in.at[core], pooled_in.at[core], 1)
     pooled_over.start()
@@ -369,6 +372,8 @@
     grad_over = core_copy(grad_out.at[1 - core], grad_core, 2)
     grad_over.start()
     item_grad_ref[...] = (dfeatures[:, E : 2 * E] + dfeatures[:, 2 * E :] * user_rows).astype(BF16)
+    item_store = pltpu.make_async_copy(item_grad_ref, item_grad_hbm, store_sem.at[0])
+    item_store.start()
     grad_over.wait_recv()
     grad_pair[...] = grad_out[core] + grad_core[...]
 
@@ -383,7 +388,7 @@
 
     lax.fori_loop(1, N_Z, send_grad, 0)
     grad_in[z] = grad_pair[z]
-    lax.fori_loop(11, 19, count_step, 0)
+    lax.fori_loop(12, 22, count_step, 0)
     lax.fori_loop(1, N_Z, wait_grad, 0)
     request_grad = jnp.sum(grad_in[...], axis=0)
     request_out[...] = request_grad
@@ -401,7 +406,7 @@
 
     for s in (4, 3, 5, 2, 6, 1, 7):
         y_copy(s).start()
-    lax.fori_loop(19, 22, count_step, 0)
+    lax.fori_loop(22, 24, count_step, 0)
     for s in range(1, N_Y):
         arrived(request_in, request_recv, (y + s) % N_Y)
     left, right = from_messages(request_in[...])
@@ -427,19 +432,33 @@
         )
 
     lax.fori_loop(1, N_Z, send_z, 0)
-    for step in range(1, N_X):
+    for step in (2, 1, 3):
         x_copy(z, x, step).start()
-    lax.fori_loop(22, 24, count_step, 0)
 
     def pass_on(s, _):
         where = wrap(z + alternate(s, N_Z), N_Z)
         block = quarter(where, x)
         pltpu.make_async_copy(block, block, z_recv.at[where]).wait()
-        for step in range(1, N_X):
+        for step in (2, 1, 3):
             x_copy(where, x, step).start()
         return 0
 
     lax.fori_loop(1, N_Z, pass_on, 0)
+
+    def drain_z(s, _):
+        z_copy(ids_all.at[z], ids_all.at[z], ids_send, ids_recv, s).wait_send()
+        z_copy(pooled_out, pooled_in.at[core, z], pooled_send, pooled_recv, s).wait_send()
+        z_copy(grad_pair.at[0], grad_in.at[z], grad_send, grad_recv, s).wait_send()
+        z_copy(quarter(z, x), quarter(z, x), z_send, z_recv, s).wait_send()
+        return 0
+
+    for s in range(1, N_Y):
+        y_copy(s).wait_send()
+    for step in ROW_STEPS:
+        row_copy(partial_out.at[0], partial_in.at[k], partial_send, partial_recv, step).wait_send()
+    lax.fori_loop(1, N_Z, drain_z, 0)
+    pooled_over.wait_send()
+    grad_over.wait_send()
 
     def product(where, side):
         columns = pl.ds(pl.multiple_of(where * GROUP, GROUP), GROUP)
@@ -465,31 +484,22 @@
     part_out[...] = (parts[1 - core] + product(last, 1 - core)).astype(BF16)
     part_over = core_copy(part_out, part_in, 3)
     part_over.start()
+
+    def drain_x(where, _):
+        for step in range(1, N_X):
+            x_copy(where, x, step).wait_send()
+        return 0
+
+    lax.fori_loop(0, N_Z, drain_x, 0)
     own_part = parts[core] + product(last, core)
     part_over.wait_recv()
     table_grad_ref[...] = own_part + part_in[...].astype(F32)
-
-    def drain_z(s, _):
-        z_copy(ids_all.at[z], ids_all.at[z], ids_send, ids_recv, s).wait_send()
-        z_copy(pooled_out, pooled_in.at[core, z], pooled_send, pooled_recv, s).wait_send()
-        z_copy(grad_pair.at[0], grad_in.at[z], grad_send, grad_recv, s).wait_send()
-        z_copy(quarter(z, x), quarter(z, x), z_send, z_recv, s).wait_send()
-        return 0
-
-    def drain_x(where, _):
-        for step in range(1, N_X):
-            x_copy(where, x, step).wait_send()
-        return 0
-
-    for s in range(1, N_Y):
-        y_copy(s).wait_send()
-    for step in ROW_STEPS:
-        row_copy(partial_out.at[0], partial_in.at[k], partial_send, partial_recv, step).wait_send()
-    lax.fori_loop(1, N_Z, drain_z, 0)
-    lax.fori_loop(0, N_Z, drain_x, 0)
+    table_store = pltpu.make_async_copy(table_grad_ref, table_grad_hbm, store_sem.at[1])
+    table_store.start()
+
     part_over.wait_send()
-    pooled_over.wait_send()
-    grad_over.wait_send()
+    table_store.wait()
+    item_store.wait()
 
 
 def hand_over(table_grad_hbm, item_grad_hbm, table_grad_out, item_grad_out, table_grad, item_grad, sem):
@@ -523,8 +533,10 @@
         kernel,
         out_shape=outs,
         in_specs=[hbm] * 8 + [vmem],
-        out_specs=(vmem, vmem),
+        out_specs=(hbm, hbm),
         scratch_shapes=[
+            pltpu.VMEM((SHARE, E), F32),
+            pltpu.VMEM((CAND, E), BF16),
             pltpu.VMEM((ROWS, E), BF16),
             pltpu.VMEM((3 * E, H), BF16),
             pltpu.VMEM((BAG, GROUP), jnp.int32),
@@ -552,6 +564,7 @@
             pltpu.VMEM((SHARE, E), BF16),
             pltpu.VMEM((SHARE, E), BF16),
             dma((8,)),
+            dma((2,)),
             dma((N_Z,)),
             dma((N_Z,)),
             dma((N_ROW,)),

time: 66.6 us -> 66.2 us (level)
  no operation moved by 1% of the time
where the time goes in v6:
time: 66.2 us; the launch traced here: 66 us
  Pallas kernels  65.3 us (99%)
    pallas_call x1, Pallas kernels, per_device(): pl.pallas_call(kernel, out_shape=outs, in_specs=[hbm] * 8 + [vmem], out_s...  63.6 us
    pallas_call x1, Pallas kernels, per_device(): pl.pallas_call(hand_over, out_shape=outs, in_specs=[hbm] * 2, out_specs=(...  1.73 us

profile of v6, /device:TPU:1, one launch (start us, length us, event | category | flops | bytes accessed | tf_op | source)
XLA Modules:
  0.0 66.0 jit_solution(2505576241331043741)
XLA Ops:
  0.6 63.6 %shard_map.104 = (f32[256,256]{1,0:T(8,128)}, bf16[256,256]{1,0:T(8,128)(2,1)}) custom-call(bf16[6144,256]{1,0:T(8,128)(2,1)} %table_hbm.1, s32[32,128]{1,0:T(8,128)} %bitcast.3, bf16[256,256]{1,0:T(8,128)(2,1)} %item_hbm.1, s32[1,96]{1,0:T(1,128)} %counts_hbm.1, s32[1,96]{1,0:T(1,128)} %placement_hbm.1, s32[1,256]{1,0:T(1,128)} %bitcast.5, ...), custom_call_target="tpu_custom_call" | custom-call | tf_op jit(solution)/shard_map/pallas_call | solution.py:532
  64.2 1.7 %shard_map.105 = (f32[256,256]{1,0:T(8,128)}, bf16[256,256]{1,0:T(8,128)(2,1)}) custom-call(f32[256,256]{1,0:T(8,128)} %get-tuple-element.4.table_grad_hbm, bf16[256,256]{1,0:T(8,128)(2,1)} %get-tuple-element.5.item_grad_hbm), custom_call_target="tpu_custom_call" | custom-call | tf_op jit(solution)/shard_map/pallas_call | solution.py:599
